TPU v7x, 128 devices: a whole 4x4x4 slice. The times are simulated.
128 devices in a mesh: frames: 16 (over x_hi, y, core), rows: 8 (over x_lo, z).
Axes of the slice: x: 4 (x_hi: 2, x_lo: 2; x = x_hi * 2 + x_lo), y: 4, z: 4, core: 2. Of those that a mesh axis runs over, the one named last changes fastest.
Arguments:
- clip: bfloat16 [32, 64, 512, 256], P('frames', 'rows'), may hold values from -6 to 6
- w_query: bfloat16 [256, 256], replicated, may hold values from -32 to 32
- w_key: bfloat16 [256, 256], replicated, may hold values from -1 to 1
- w_value: bfloat16 [256, 256], replicated, may hold values from -0.375 to 0.375
- w_out: bfloat16 [256, 256], replicated, may hold values from -0.375 to 0.375
- w_conv: bfloat16 [3, 3, 256, 256], replicated, may hold values from -0.125 to 0.125
- conv_bias: float32 [256], replicated, may hold values from -3 to 3
Outputs:
- upsampled: bfloat16 [32, 128, 512, 128], P('frames', 'rows')
All inputs are finite; a program needn't handle non-finite values.
Results may differ from a plain program's by a relative error of at most 0.012.
Values may be sent and summed in bfloat16 or wider, within the bound.
No kernel may reach another device: no remote copies, remote signals or barrier semaphores. Data moves between devices by JAX's collectives and lax.ppermute only.
A program may use at most 192 MiB of HBM per device.

v0:
```python
import jax
import jax.numpy as jnp
import numpy as np
from jax import lax
from jax.experimental import pallas as pl
from jax.experimental.pallas import tpu as pltpu
from jax.sharding import PartitionSpec as P

HEADS = 8
HEAD = 32
FRAMES = 32
C = 256
GROUP = 8
F32 = jnp.float32
BF16 = jnp.bfloat16


def dot(a, b):
    return jnp.dot(a, b, preferred_element_type=F32)


def dot_nt(a, b):
    return lax.dot_general(a, b, (((1,), (1,)), ((), ())), preferred_element_type=F32)


def group_max(s):
    halves = []
    for i in range(s.shape[1] // 128):
        m = s[:, 128 * i : 128 * (i + 1)]
        lanes = lax.broadcasted_iota(jnp.int32, m.shape, 1)
        for step in (1, 2, 4, 8, 16):
            m = jnp.maximum(m, jnp.take_along_axis(m, lanes ^ step, axis=1))
        halves.append(m)
    return jnp.concatenate(halves, axis=1)


def attention_kernel(x_ref, wq_ref, wk_ref, wv_ref, wo_ref, perm_ref, back_ref, same_ref, out_ref):
    pixels = x_ref.shape[1]
    x = x_ref[...].astype(F32)
    mean = jnp.mean(x, axis=-1, keepdims=True)
    centred = x - mean
    var = jnp.mean(centred * centred, axis=-1, keepdims=True)
    normed = centred * lax.rsqrt(var + 1e-6)
    rows = GROUP * FRAMES
    parts = []
    for j in range(pixels // GROUP):
        part = normed[:, j * GROUP : (j + 1) * GROUP].reshape(rows, C).astype(BF16)
        parts.append(dot(perm_ref[...], part).astype(BF16))
    xp = jnp.concatenate(parts, axis=0)
    q = dot(xp, wq_ref[...]).astype(BF16)
    k = dot(xp, wk_ref[...]).astype(BF16)
    v = dot(xp, wv_ref[...]).astype(BF16)
    same = same_ref[...]
    scores = []
    for p in range(pixels):
        at = slice(p * FRAMES, (p + 1) * FRAMES)
        scores.append(dot_nt(q[at], jnp.concatenate([k[at]] * HEADS, axis=0) * same))
    s = jnp.concatenate(scores, axis=0)
    factor = np.float32(np.log2(np.e) / np.sqrt(HEAD))
    e = jnp.exp2((s - group_max(s)) * factor).astype(BF16)
    total = dot(e, same)
    sums = []
    for p in range(pixels):
        at = slice(p * FRAMES, (p + 1) * FRAMES)
        sums.append(dot(e[at], jnp.concatenate([v[at]] * HEADS, axis=0) * same))
    attended = (jnp.concatenate(sums, axis=0) / total).astype(BF16)
    projected = dot(attended, wo_ref[...]).astype(BF16)
    for j in range(pixels // GROUP):
        part = dot(back_ref[...], projected[j * rows : (j + 1) * rows])
        parts[j] = part.reshape(FRAMES, GROUP, C)
    out_ref[...] = jnp.concatenate(parts, axis=1).astype(BF16)


def attention(x, wq, wk, wv, wo, pixels=16):
    count = x.shape[1]
    row = np.arange(GROUP * FRAMES)
    source = (row % FRAMES) * GROUP + row // FRAMES
    perm = (source[:, None] == row[None, :]).astype(np.float32)
    same = (row[:, None] // HEAD == row[None, :] // HEAD).astype(np.float32)
    whole = pl.BlockSpec((C, C), lambda i: (0, 0))
    block = pl.BlockSpec((FRAMES, pixels, C), lambda i: (0, i, 0))
    tokens = FRAMES * count
    return pl.pallas_call(
        attention_kernel,
        out_shape=jax.ShapeDtypeStruct(x.shape, BF16),
        grid=(count // pixels,),
        in_specs=[block] + [whole] * 7,
        out_specs=block,
        compiler_params=pltpu.CompilerParams(vmem_limit_bytes=48 * 2**20),
        cost_estimate=pl.CostEstimate(
            flops=2 * tokens * C * C * 8, bytes_accessed=4 * tokens * C, transcendentals=tokens * C
        ),
        name="attention",
    )(x, wq, wk, wv, wo, jnp.asarray(perm, BF16), jnp.asarray(perm.T, BF16), jnp.asarray(same, BF16))


def silu(v):
    return v / (1.0 + jnp.exp(-v))


def conv_kernel(clip_ref, proj_ref, up_ref, down_ref, w_ref, bias_ref, out_ref, act_ref, hid_ref):
    rows, width = clip_ref.shape[1], clip_ref.shape[2]
    pix = lax.broadcasted_iota(jnp.int32, (width, C), 0)

    def put(row, act):
        before = jnp.where(pix == 0, 0.0, pltpu.roll(act, 1, 0))
        after = jnp.where(pix == width - 1, 0.0, pltpu.roll(act, width - 1, 0))
        act_ref[row, :, 0:C] = before.astype(BF16)
        act_ref[row, :, C : 2 * C] = act.astype(BF16)
        act_ref[row, :, 2 * C :] = after.astype(BF16)

    def load(r):
        p = jnp.concatenate([proj_ref[2 * r, 0], proj_ref[2 * r + 1, 0]], axis=0)
        hidden = clip_ref[0, r].astype(F32) + p.astype(F32)
        hid_ref[r % 2] = hidden
        put(r + 1, silu(hidden).astype(BF16).astype(F32))

    put(0, up_ref[0, 0].astype(F32))
    load(0)
    for r in range(rows):
        if r + 1 < rows:
            load(r + 1)
        else:
            put(rows + 1, down_ref[0, 0].astype(F32))
        acc = hid_ref[r % 2] + bias_ref[...]
        for dy in range(3):
            acc = acc + dot(act_ref[r + dy], w_ref[dy])
        mixed = acc.astype(BF16)
        out_ref[0, 2 * r] = mixed[:, : C // 2]
        out_ref[0, 2 * r + 1] = mixed[:, C // 2 :]


def conv(clip, proj, up, down, w, bias):
    frames, rows, width, _ = clip.shape
    return pl.pallas_call(
        conv_kernel,
        out_shape=jax.ShapeDtypeStruct((frames, 2 * rows, width, C // 2), BF16),
        grid=(frames,),
        in_specs=[
            pl.BlockSpec((1, rows, width, C), lambda f: (f, 0, 0, 0)),
            pl.BlockSpec((2 * rows, 1, width // 2, C), lambda f: (0, f, 0, 0)),
            pl.BlockSpec((1, 1, width, C), lambda f: (f, 0, 0, 0)),
            pl.BlockSpec((1, 1, width, C), lambda f: (f, 0, 0, 0)),
            pl.BlockSpec((3, 3 * C, C), lambda f: (0, 0, 0)),
            pl.BlockSpec((1, C), lambda f: (0, 0)),
        ],
        out_specs=pl.BlockSpec((1, 2 * rows, width, C // 2), lambda f: (f, 0, 0, 0)),
        scratch_shapes=[
            pltpu.VMEM((rows + 2, width, 3 * C), BF16),
            pltpu.VMEM((2, width, C), F32),
        ],
        compiler_params=pltpu.CompilerParams(vmem_limit_bytes=56 * 2**20),
        cost_estimate=pl.CostEstimate(
            flops=2 * frames * rows * width * 9 * C * C,
            bytes_accessed=6 * frames * rows * width * C,
            transcendentals=frames * rows * width * C,
        ),
        name="residual_conv",
    )(clip, proj, up, down, w.reshape(3, 3 * C, C), bias.reshape(1, C))


def local(clip, w_query, w_key, w_value, w_out, w_conv, conv_bias):
    frames, rows, width, chans = clip.shape
    n = lax.axis_size("frames")
    share = rows * width // n
    cut = clip.reshape(frames, n, share, chans).transpose(1, 0, 2, 3)
    got = lax.all_to_all(cut, "frames", split_axis=0, concat_axis=0, tiled=True)
    proj = attention(got.reshape(n * frames, share, chans), w_query, w_key, w_value, w_out)
    proj = proj.reshape(n, frames, share, chans)
    proj = lax.all_to_all(proj, "frames", split_axis=0, concat_axis=0, tiled=True)
    per = width // share

    def edge(r):
        p = proj[r * per : (r + 1) * per].transpose(1, 0, 2, 3).reshape(frames, 1, width, chans)
        hidden = clip[:, r : r + 1].astype(F32) + p.astype(F32)
        return silu(hidden).astype(BF16)

    size = lax.axis_size("rows")
    up = lax.ppermute(edge(rows - 1), "rows", [(i, i + 1) for i in range(size - 1)])
    down = lax.ppermute(edge(0), "rows", [(i + 1, i) for i in range(size - 1)])
    return conv(clip, proj, up, down, w_conv, conv_bias)


def solution(mesh):
    placed = (P("frames", "rows", None, None), P(), P(), P(), P(), P(), P())
    return jax.shard_map(
        local,
        mesh=mesh,
        in_specs=placed,
        out_specs=P("frames", "rows", None, None),
        check_vma=False,
    )
```

profile of v0, /device:TPU:10, one launch (start us, length us, event | category | flops | bytes accessed | tf_op | source)
XLA Modules:
  0.0 203.0 jit_solution(8985649838569430907)
XLA Ops:
  0.0 2.5 %copy.15 = bf16[2,16,256,256]{3,2,0,1:T(8,128)(2,1)S(1)} copy(bf16[2,16,256,256]{3,2,1,0:T(8,128)(2,1)} %bitcast.23) | data formatting | bytes 8388608 | tf_op jit(solution)/shard_map/reshape | solution.py:166
  2.5 0.0 copy-start
  2.5 0.0 copy-start.1
  2.5 0.0 copy-start.2
  2.5 0.0 copy-start.3
  2.5 0.0 copy-start.4
  2.5 0.0 copy-start.5
  2.5 0.0 copy-start.6
  2.5 54.7 %all_to_all.10 = bf16[16,2,256,256]{3,2,1,0:T(8,128)(2,1)} all-to-all(bf16[16,2,256,256]{3,2,1,0:T(8,128)(2,1)S(1)} %bitcast.22), channel_id=1, replica_groups=mesh['frames'=16,'rows'=8] {'frames'}, dimensions={0} | all-to-all | bytes 8388608 | tf_op jit(solution)/shard_map/all_to_all | solution.py:167
  57.2 0.0 copy-done
  57.2 0.0 copy-done.1
  57.2 0.0 copy-done.2
  57.2 0.0 copy-done.3
  57.2 0.0 copy-done.4
  57.2 0.0 copy-done.5
  57.2 0.0 copy-done.6
  57.3 47.9 %attention.1 = bf16[32,256,256]{2,1,0:T(8,128)(2,1)S(1)} custom-call(bf16[32,256,256]{2,1,0:T(8,128)(2,1)} %bitcast.24, bf16[256,256]{1,0:T(8,128)(2,1)S(1)} %copy-done, bf16[256,256]{1,0:T(8,128)(2,1)S(1)} %copy-done.1, bf16[256,256]{1,0:T(8,128)(2,1)S(1)} %copy-done.2, bf16[256,256]{1,0:T(8,128)(2,1)S(1)} %copy-done.3, bf16[256,256]{1,0:T(8,128)(2,1)S(1)} %copy-done.6, ...), custom_call_target="tpu_custom_call" | custom-call | flops 8589934592 | bytes 8388608 | tf_op jit(solution)/shard_map/attention/pallas_call | solution.py:83
  105.2 54.3 %all_to_all.11.proj_ref = bf16[16,2,256,256]{3,2,1,0:T(8,128)(2,1)S(1)} all-to-all(bf16[16,2,256,256]{3,2,1,0:T(8,128)(2,1)S(1)} %bitcast.21), channel_id=1, replica_groups=mesh['frames'=16,'rows'=8] {'frames'}, dimensions={0} | all-to-all | bytes 8388608 | tf_op jit(solution)/shard_map/all_to_all | solution.py:170
  159.5 0.0 copy-start.7
  159.5 0.2 convert_bitcast_fusion
  159.7 0.1 copy.13
  159.8 0.1 copy.12
  159.9 2.7 %divide_convert_fusion = (bf16[2,1,512,256]{3,2,1,0:T(8,128)(2,1)S(1)}, bf16[2,1,512,256]{3,2,1,0:T(8,128)(2,1)S(1)}) fusion(bf16[2,8,512,256]{3,2,1,0:T(8,128)(2,1)} %clip_ref.1, f32[2,1,512,256]{3,2,1,0:T(8,128)S(1)} %bitcast.25, f32[2,1,512,256]{3,2,1,0:T(8,128)S(1)} %bitcast.26), kind=kLoop, calls=%fused_computation.5 | loop fusion | flops 3145728 | bytes 4194304 | tf_op jit(solution)/shard_map/convert_element_type | solution.py:176
  162.6 0.0 copy-done.7
  162.6 6.8 %collective-permute-start.1 = (bf16[2,1,512,256]{3,2,1,0:T(8,128)(2,1)S(1)}, bf16[2,1,512,256]{3,2,1,0:T(8,128)(2,1)S(1)}, u32[]{:S(2)}, u32[]{:S(2)}) collective-permute-start(bf16[2,1,512,256]{3,2,1,0:T(8,128)(2,1)S(1)} %get-tuple-element.5), channel_id=1, source_target_pairs={{1,0},{2,1},{3,2},{4,3},{5,4},{6,5},{7,6},{9,8},{10,9},{11,10},{12... | collective-permute-start | bytes 1572872 | tf_op jit(solution)/shard_map/ppermute | solution.py:180
  169.4 1.9 collective-permute-start
  171.3 10.2 %collective-permute-done.1.down_ref = bf16[2,1,512,256]{3,2,1,0:T(8,128)(2,1)S(1)} collective-permute-done((bf16[2,1,512,256]{3,2,1,0:T(8,128)(2,1)S(1)}, bf16[2,1,512,256]{3,2,1,0:T(8,128)(2,1)S(1)}, u32[]{:S(2)}, u32[]{:S(2)}) %collective-permute-start.1) | collective-permute-done | bytes 524320 | tf_op jit(solution)/shard_map/ppermute | solution.py:180
  181.5 0.0 copy-start.8
  181.5 6.2 %collective-permute-done.up_ref = bf16[2,1,512,256]{3,2,1,0:T(8,128)(2,1)S(1)} collective-permute-done((bf16[2,1,512,256]{3,2,1,0:T(8,128)(2,1)S(1)}, bf16[2,1,512,256]{3,2,1,0:T(8,128)(2,1)S(1)}, u32[]{:S(2)}, u32[]{:S(2)}) %collective-permute-start) | collective-permute-done | bytes 524320 | tf_op jit(solution)/shard_map/ppermute | solution.py:179
  187.7 0.0 copy-start.9
  187.7 0.0 copy-done.8
  187.7 0.8 copy-done.9
  188.5 14.5 %residual_conv.1 = bf16[2,16,512,128]{3,2,1,0:T(8,128)(2,1)} custom-call(bf16[2,8,512,256]{3,2,1,0:T(8,128)(2,1)} %clip_ref.1, bf16[16,2,256,256]{3,2,1,0:T(8,128)(2,1)} %copy-done.7, bf16[2,1,512,256]{3,2,1,0:T(8,128)(2,1)} %copy-done.9, bf16[2,1,512,256]{3,2,1,0:T(8,128)(2,1)} %copy-done.8, bf16[3,768,256]{2,1,0:T(8,128)(2,1)} %bitcast.27, f32[1,256]{1,0:T(1,128)} %bitcast.28), custom_call_target="tpu_custom_call" | custom-call | flops 9663676416 | bytes 12582912 | tf_op jit(solution)/shard_map/residual_conv/pallas_call | solution.py:135
Async XLA Ops:
  2.5 54.7 %copy-start = (bf16[256,256]{1,0:T(8,128)(2,1)S(1)}, bf16[256,256]{1,0:T(8,128)(2,1)}, u32[]{:S(2)}) copy-start(bf16[256,256]{1,0:T(8,128)(2,1)} %wq_ref.1) | copy-start | bytes 393220
  2.5 54.7 %copy-start.1 = (bf16[256,256]{1,0:T(8,128)(2,1)S(1)}, bf16[256,256]{1,0:T(8,128)(2,1)}, u32[]{:S(2)}) copy-start(bf16[256,256]{1,0:T(8,128)(2,1)} %wk_ref.1) | copy-start | bytes 393220
  2.5 54.7 %copy-start.2 = (bf16[256,256]{1,0:T(8,128)(2,1)S(1)}, bf16[256,256]{1,0:T(8,128)(2,1)}, u32[]{:S(2)}) copy-start(bf16[256,256]{1,0:T(8,128)(2,1)} %wv_ref.1) | copy-start | bytes 393220
  2.5 54.7 %copy-start.3 = (bf16[256,256]{1,0:T(8,128)(2,1)S(1)}, bf16[256,256]{1,0:T(8,128)(2,1)}, u32[]{:S(2)}) copy-start(bf16[256,256]{1,0:T(8,128)(2,1)} %wo_ref.1) | copy-start | bytes 393220
  2.5 54.7 %copy-start.4 = (bf16[256,256]{1,0:T(8,128)(2,1)S(1)}, bf16[256,256]{1,0:T(8,128)(2,1)}, u32[]{:S(2)}) copy-start(bf16[256,256]{1,0:T(8,128)(2,1)} %constant.10.clone.same_ref) | copy-start | bytes 393220
  2.5 54.7 %copy-start.5 = (bf16[256,256]{1,0:T(8,128)(2,1)S(1)}, bf16[256,256]{1,0:T(8,128)(2,1)}, u32[]{:S(2)}) copy-start(bf16[256,256]{1,0:T(8,128)(2,1)} %constant.9.clone.back_ref) | copy-start | bytes 393220
  2.5 54.7 %copy-start.6 = (bf16[256,256]{1,0:T(8,128)(2,1)S(1)}, bf16[256,256]{1,0:T(8,128)(2,1)}, u32[]{:S(2)}) copy-start(bf16[256,256]{1,0:T(8,128)(2,1)} %constant.8.clone.perm_ref) | copy-start | bytes 393220
  159.5 3.1 %copy-start.7 = (bf16[16,2,256,256]{3,2,1,0:T(8,128)(2,1)}, bf16[16,2,256,256]{3,2,1,0:T(8,128)(2,1)S(1)}, u32[]{:S(2)}) copy-start(bf16[16,2,256,256]{3,2,1,0:T(8,128)(2,1)S(1)} %all_to_all.11.proj_ref) | copy-start | bytes 12582916
  162.6 18.9 %collective-permute-start.1 = (bf16[2,1,512,256]{3,2,1,0:T(8,128)(2,1)S(1)}, bf16[2,1,512,256]{3,2,1,0:T(8,128)(2,1)S(1)}, u32[]{:S(2)}, u32[]{:S(2)}) collective-permute-start(bf16[2,1,512,256]{3,2,1,0:T(8,128)(2,1)S(1)} %get-tuple-element.5), channel_id=1, source_target_pairs={{1,0},{2,1},{3,2},{4,3},{5,4},{6,5},{7,6},{9,8},{10,9},{11,10},{12... | collective-permute-start | bytes 1572872 | tf_op jit(solution)/shard_map/ppermute | solution.py:180
  169.4 18.3 %collective-permute-start = (bf16[2,1,512,256]{3,2,1,0:T(8,128)(2,1)S(1)}, bf16[2,1,512,256]{3,2,1,0:T(8,128)(2,1)S(1)}, u32[]{:S(2)}, u32[]{:S(2)}) collective-permute-start(bf16[2,1,512,256]{3,2,1,0:T(8,128)(2,1)S(1)} %get-tuple-element.6), channel_id=1, source_target_pairs={{0,1},{1,2},{2,3},{3,4},{4,5},{5,6},{6,7},{8,9},{9,10},{10,11},{11... | collective-permute-start | bytes 1572872 | tf_op jit(solution)/shard_map/ppermute | solution.py:179
  181.5 6.2 %copy-start.8 = (bf16[2,1,512,256]{3,2,1,0:T(8,128)(2,1)}, bf16[2,1,512,256]{3,2,1,0:T(8,128)(2,1)S(1)}, u32[]{:S(2)}) copy-start(bf16[2,1,512,256]{3,2,1,0:T(8,128)(2,1)S(1)} %collective-permute-done.1.down_ref) | copy-start | bytes 1572868
  187.7 0.8 copy-start.9
where the time goes:
time: 205 us; the launch traced here: 203 us
  blocking collectives  109 us (53%)
  Pallas kernels  62.4 us (30%)
  waiting for transfers between devices  16.4 us (8%)
  starting transfers between devices  8.72 us (4%)
  local copies, waits for them, and re-layouts  3.44 us (2%)
  other arithmetic  2.87 us (1%)
    all_to_all x1, blocking collectives, local(): got = lax.all_to_all(cut, 'frames', split_axis=0, concat_axis=0, tiled=True)  54.7 us
    all_to_all x1, blocking collectives, local(): lax.all_to_all(proj, 'frames', split_axis=0, concat_axis=0, tiled=True)  54.3 us
    pallas_call x1, Pallas kernels, attention(): pl.pallas_call(attention_kernel, out_shape=jax.ShapeDtypeStruct(x.shape,...  47.9 us
    pallas_call x1, Pallas kernels, conv(): pl.pallas_call(conv_kernel, out_shape=jax.ShapeDtypeStruct((frames, 2 * r...  14.5 us
    ppermute x1, waiting for transfers between devices, local(): down = lax.ppermute(edge(0), 'rows', [(i + 1, i) for i in range(size - 1)])  10.2 us
    ppermute x1, starting transfers between devices, local(): down = lax.ppermute(edge(0), 'rows', [(i + 1, i) for i in range(size - 1)])  6.8 us
    ppermute x1, waiting for transfers between devices, local(): lax.ppermute(edge(rows - 1), 'rows', [(i, i + 1) for i in range(size - 1)])  6.22 us
  transfers between devices with their start and end apart: 2, of which 2 were waited for; matrix products, arithmetic and copies ran while one was open for 0% of the time, Pallas kernels for 0%

commit v1 on v0

v1 whole, which is shorter than its diff:
```python
import functools

import jax
import jax.numpy as jnp
import numpy as np
from jax import lax
from jax.experimental import pallas as pl
from jax.experimental.pallas import tpu as pltpu
from jax.sharding import PartitionSpec as P

HEADS = 8
HEAD = 32
FRAMES = 32
C = 256
GROUP = 8
VMEM = 60 * 2**20
F32 = jnp.float32
BF16 = jnp.bfloat16


def dot(a, b):
    return jnp.dot(a, b, preferred_element_type=F32)


def dot_nt(a, b):
    return lax.dot_general(a, b, (((1,), (1,)), ((), ())), preferred_element_type=F32)


def group_max(s):
    t = s.T
    rows = t.shape[1]
    m = jnp.max(t.reshape(HEADS, HEAD, rows), axis=1, keepdims=True)
    return jnp.broadcast_to(m, (HEADS, HEAD, rows)).reshape(C, rows).T


def attention_kernel(parts_in, slots_ref, *refs):
    x_refs = refs[:parts_in]
    wq_ref, wk_ref, wv_ref, wo_ref, perm_ref, back_ref, same_ref = refs[parts_in : parts_in + 7]
    out_ref = refs[-1]
    pixels = x_refs[0].shape[-2]
    x = jnp.concatenate([r[...].reshape(-1, pixels, C) for r in x_refs], axis=0).astype(F32)
    mean = jnp.mean(x, axis=-1, keepdims=True)
    centred = x - mean
    var = jnp.mean(centred * centred, axis=-1, keepdims=True)
    normed = centred * lax.rsqrt(var + 1e-6)
    rows = GROUP * FRAMES
    parts = []
    for j in range(pixels // GROUP):
        part = normed[:, j * GROUP : (j + 1) * GROUP].reshape(rows, C).astype(BF16)
        parts.append(dot(perm_ref[...], part).astype(BF16))
    xp = jnp.concatenate(parts, axis=0)
    q = dot(xp, wq_ref[...]).astype(BF16)
    k = dot(xp, wk_ref[...]).astype(BF16)
    v = dot(xp, wv_ref[...]).astype(BF16)
    same = same_ref[...]
    scores = []
    for p in range(pixels):
        at = slice(p * FRAMES, (p + 1) * FRAMES)
        scores.append(dot_nt(q[at], jnp.concatenate([k[at]] * HEADS, axis=0) * same))
    s = jnp.concatenate(scores, axis=0)
    factor = np.float32(np.log2(np.e) / np.sqrt(HEAD))
    e = jnp.exp2((s - group_max(s)) * factor).astype(BF16)
    total = dot(e, same)
    sums = []
    for p in range(pixels):
        at = slice(p * FRAMES, (p + 1) * FRAMES)
        sums.append(dot(e[at], jnp.concatenate([v[at]] * HEADS, axis=0) * same))
    attended = (jnp.concatenate(sums, axis=0) / total).astype(BF16)
    projected = dot(attended, wo_ref[...]).astype(BF16)
    for j in range(pixels // GROUP):
        part = dot(back_ref[...], projected[j * rows : (j + 1) * rows])
        parts[j] = part.reshape(FRAMES, GROUP, C)
    out = jnp.concatenate(parts, axis=1).astype(BF16)
    for i in range(FRAMES // 2):
        out_ref[slots_ref[i]] = out[2 * i : 2 * i + 2]


def attention(slots, xs, weights, pixels, cost):
    count = xs[0].shape[-2]
    row = np.arange(GROUP * FRAMES)
    source = (row % FRAMES) * GROUP + row // FRAMES
    perm = (source[:, None] == row[None, :]).astype(np.float32)
    same = (row[:, None] // HEAD == row[None, :] // HEAD).astype(np.float32)
    whole = pl.BlockSpec((C, C), lambda i, s: (0, 0))
    blocks = []
    for x in xs:
        if x.ndim == 3:
            blocks.append(pl.BlockSpec((x.shape[0], pixels, C), lambda i, s: (0, i, 0)))
        else:
            shape = (x.shape[0], 1, x.shape[2], pixels, C)
            blocks.append(pl.BlockSpec(shape, lambda i, s: (0, s[FRAMES // 2], 0, i, 0)))
    pairs = FRAMES // 2
    return pl.pallas_call(
        functools.partial(attention_kernel, len(xs)),
        out_shape=jax.ShapeDtypeStruct((pairs, 2, count, C), BF16),
        grid_spec=pltpu.PrefetchScalarGridSpec(
            num_scalar_prefetch=1,
            grid=(count // pixels,),
            in_specs=blocks + [whole] * 7,
            out_specs=pl.BlockSpec((pairs, 2, pixels, C), lambda i, s: (0, 0, i, 0)),
        ),
        compiler_params=pltpu.CompilerParams(vmem_limit_bytes=VMEM),
        cost_estimate=pl.CostEstimate(flops=cost, bytes_accessed=cost // 1000, transcendentals=0),
        name="attention",
    )(slots, *xs, *weights, jnp.asarray(perm, BF16), jnp.asarray(perm.T, BF16), jnp.asarray(same, BF16))


def silu(v):
    return v / (1.0 + jnp.exp(-v))


EARLY = (0, 3)
LATE = (1, 2)


def hidden_row(clip_refs, proj_ref, i):
    p = jnp.concatenate([proj_ref[4 * i + j, 0] for j in range(4)], axis=0)
    return clip_refs[i // 2][0, i % 2].astype(F32) + p.astype(F32)


def put(act_ref, slot, act):
    width = act.shape[0]
    pix = lax.broadcasted_iota(jnp.int32, act.shape, 0)
    before = jnp.where(pix == 0, 0.0, pltpu.roll(act, 1, 0))
    after = jnp.where(pix == width - 1, 0.0, pltpu.roll(act, width - 1, 0))
    act_ref[slot, :, 0:C] = before.astype(BF16)
    act_ref[slot, :, C : 2 * C] = act.astype(BF16)
    act_ref[slot, :, 2 * C :] = after.astype(BF16)


def activate(hidden):
    return silu(hidden).astype(BF16).astype(F32)


def early_kernel(top_ref, bottom_ref, proj_ref, w_ref, bias_ref, part_ref, last_ref, lead_ref, act_ref):
    bias = bias_ref[...]

    def load(i):
        hidden = hidden_row((top_ref, bottom_ref), proj_ref, i)
        put(act_ref, i, activate(hidden))
        return hidden + bias

    first = load(0)
    second = load(1)
    part_ref[0, 0] = first + dot(act_ref[0], w_ref[1]) + dot(act_ref[1], w_ref[2])
    sixth = load(2)
    part_ref[0, 1] = second + dot(act_ref[0], w_ref[0]) + dot(act_ref[1], w_ref[1])
    part_ref[0, 2] = dot(act_ref[1], w_ref[0])
    seventh = load(3)
    part_ref[0, 3] = dot(act_ref[2], w_ref[2])
    part_ref[0, 4] = sixth + dot(act_ref[2], w_ref[1]) + dot(act_ref[3], w_ref[2])
    part_ref[0, 5] = seventh + dot(act_ref[2], w_ref[0]) + dot(act_ref[3], w_ref[1])
    last_ref[0, 0] = act_ref[3, :, C : 2 * C]
    lead_ref[0, 0] = act_ref[0, :, C : 2 * C]


def late_kernel(top_ref, bottom_ref, proj_ref, up_ref, down_ref, part_ref, w_ref, bias_ref, out_ref, act_ref, hid_ref):
    bias = bias_ref[...]

    def load(i):
        hidden = hidden_row((top_ref, bottom_ref), proj_ref, i)
        hid_ref[i] = hidden + bias
        put(act_ref, i, activate(hidden))

    def finish(row, acc):
        mixed = acc.astype(BF16)
        out_ref[0, 2 * row] = mixed[:, : C // 2]
        out_ref[0, 2 * row + 1] = mixed[:, C // 2 :]

    put(act_ref, 4, up_ref[0, 0].astype(F32))
    load(0)
    finish(0, part_ref[0, 0] + dot(act_ref[4], w_ref[0]))
    load(1)
    finish(1, part_ref[0, 1] + dot(act_ref[0], w_ref[2]))
    load(2)
    finish(2, part_ref[0, 2] + hid_ref[0] + dot(act_ref[0], w_ref[1]) + dot(act_ref[1], w_ref[2]))
    load(3)
    for row in (3, 4):
        acc = hid_ref[row - 2]
        for dy in range(3):
            acc = acc + dot(act_ref[row - 3 + dy], w_ref[dy])
        finish(row, acc)
    put(act_ref, 5, down_ref[0, 0].astype(F32))
    finish(5, part_ref[0, 3] + hid_ref[3] + dot(act_ref[2], w_ref[0]) + dot(act_ref[3], w_ref[1]))
    finish(6, part_ref[0, 4] + dot(act_ref[3], w_ref[0]))
    finish(7, part_ref[0, 5] + dot(act_ref[5], w_ref[2]))


def row_pair(clip, i):
    return pl.BlockSpec((1, 2) + clip.shape[2:], lambda f: (f, i, 0, 0))


def per_frame(shape):
    zeros = (0,) * (len(shape) - 1)
    return pl.BlockSpec((1,) + shape[1:], lambda f: (f,) + zeros)


def conv_specs(width, places, share):
    return (
        pl.BlockSpec((places, 1, share, C), lambda f: (0, f, 0, 0)),
        pl.BlockSpec((3, 3 * C, C), lambda f: (0, 0, 0)),
        pl.BlockSpec((1, C), lambda f: (0, 0)),
    )


def cost(frames, rows, width):
    return pl.CostEstimate(
        flops=2 * frames * rows * width * 9 * C * C,
        bytes_accessed=8 * frames * rows * width * C,
        transcendentals=frames * rows * width * C,
    )


def conv_early(clip, proj, w, bias):
    frames, rows, width, _ = clip.shape
    proj_spec, w_spec, bias_spec = conv_specs(width, proj.shape[0], proj.shape[2])
    edge = jax.ShapeDtypeStruct((frames, 1, width, C), BF16)
    outs = (jax.ShapeDtypeStruct((frames, 6, width, C), F32), edge, edge)
    return pl.pallas_call(
        early_kernel,
        out_shape=outs,
        grid=(frames,),
        in_specs=[row_pair(clip, EARLY[0]), row_pair(clip, EARLY[1]), proj_spec, w_spec, bias_spec],
        out_specs=tuple(per_frame(o.shape) for o in outs),
        scratch_shapes=[pltpu.VMEM((4, width, 3 * C), BF16)],
        compiler_params=pltpu.CompilerParams(vmem_limit_bytes=VMEM),
        cost_estimate=cost(frames, 4, width),
        name="conv_early",
    )(clip, clip, proj, w, bias)


def conv_late(clip, proj, up, down, part, w, bias):
    frames, rows, width, _ = clip.shape
    proj_spec, w_spec, bias_spec = conv_specs(width, proj.shape[0], proj.shape[2])
    out = jax.ShapeDtypeStruct((frames, 2 * rows, width, C // 2), BF16)
    return pl.pallas_call(
        late_kernel,
        out_shape=out,
        grid=(frames,),
        in_specs=[
            row_pair(clip, LATE[0]),
            row_pair(clip, LATE[1]),
            proj_spec,
            per_frame(up.shape),
            per_frame(down.shape),
            per_frame(part.shape),
            w_spec,
            bias_spec,
        ],
        out_specs=per_frame(out.shape),
        scratch_shapes=[pltpu.VMEM((6, width, 3 * C), BF16), pltpu.VMEM((4, width, C), F32)],
        compiler_params=pltpu.CompilerParams(vmem_limit_bytes=VMEM),
        cost_estimate=cost(frames, 4, width),
        name="conv_late",
    )(clip, clip, proj, up, down, part, w, bias)


def early_cut_kernel(clip_ref, out_ref):
    for f in range(out_ref.shape[2]):
        out_ref[:, :, f] = clip_ref[f]


def early_cut(clip, owners):
    frames, rows, width, _ = clip.shape
    share = 4 * width // owners
    runs = width // share
    return pl.pallas_call(
        early_cut_kernel,
        out_shape=jax.ShapeDtypeStruct((4, runs, frames, share, C), BF16),
        grid=(2,),
        in_specs=[pl.BlockSpec((frames, 2, runs, share, C), lambda i: (0, EARLY[1] * i, 0, 0, 0))],
        out_specs=pl.BlockSpec((2, runs, frames, share, C), lambda i: (i, 0, 0, 0, 0)),
        compiler_params=pltpu.CompilerParams(vmem_limit_bytes=VMEM),
        cost_estimate=pl.CostEstimate(flops=1000, bytes_accessed=1000, transcendentals=0),
        name="early_cut",
    )(clip.reshape(frames, rows, runs, share, C)).reshape(owners, frames, share, C)


def late_cut_kernel(half_ref, near_ref, far_ref, mine_ref, away_ref):
    mine_ref[:, :, 0] = near_ref[0]
    away_ref[:, :, 0] = far_ref[0]


def late_cut(half, clip, owners):
    frames, rows, width, _ = clip.shape
    share = 4 * width // owners
    runs = width // share
    out = jax.ShapeDtypeStruct((2, runs, frames, share, C), BF16)
    block = (1, 2, runs, share, C)
    out_spec = pl.BlockSpec((2, runs, 1, share, C), lambda f, s: (0, 0, f, 0, 0))
    clip = clip.reshape(frames, rows, runs, share, C)
    outs = pl.pallas_call(
        late_cut_kernel,
        out_shape=(out, out),
        grid_spec=pltpu.PrefetchScalarGridSpec(
            num_scalar_prefetch=1,
            grid=(frames,),
            in_specs=[
                pl.BlockSpec(block, lambda f, s: (f, LATE[0] + s[0], 0, 0, 0)),
                pl.BlockSpec(block, lambda f, s: (f, LATE[1] - s[0], 0, 0, 0)),
            ],
            out_specs=(out_spec, out_spec),
        ),
        compiler_params=pltpu.CompilerParams(vmem_limit_bytes=VMEM),
        cost_estimate=pl.CostEstimate(flops=1000, bytes_accessed=1000, transcendentals=0),
        name="late_cut",
    )(half, clip, clip)
    return [o.reshape(owners // 4, 2, frames, share, C) for o in outs]


CHIPS = 8


def exchange(a):
    return lax.all_to_all(a, "frames", split_axis=0, concat_axis=0, tiled=True)


def to_chip(a, k):
    pairs = []
    for i in range(2 * CHIPS):
        x, y, core = i // 8, i // 2 % 4, i % 2
        pairs.append((i, ((x + core) % 2 * 4 + (y + k) % 4) * 2 + core))
    return lax.ppermute(a, "frames", pairs)


def to_sibling(a):
    return lax.ppermute(a, "frames", [(i, i ^ 1) for i in range(2 * CHIPS)])


def pick(a, i, axis=0):
    return lax.dynamic_index_in_dim(a, i, axis, keepdims=False)


def local(clip, w_query, w_key, w_value, w_out, w_conv, conv_bias):
    weights = (w_query, w_key, w_value, w_out)
    frames, rows, width, chans = clip.shape
    me = lax.axis_index("frames")
    x, y, core = me // 8, me // 2 % 4, me % 2
    other = 1 - core
    w = w_conv.reshape(3, 3 * C, C)
    bias = conv_bias.reshape(1, C)

    early, clip_late = lax.optimization_barrier((early_cut(clip, 2 * CHIPS), clip))
    early = exchange(early)
    share = early.shape[2]
    early = early.reshape(FRAMES, share, chans)

    mine, away = late_cut(((x + core) % 2).astype(jnp.int32).reshape(1), clip_late, 2 * CHIPS)
    theirs = to_sibling(away)
    got = []
    for k in range(4):
        to = (y + k) % 4
        got.append(to_chip(jnp.stack([pick(mine, to), pick(theirs, to)]), k))

    order = jnp.arange(2 * CHIPS + 1, dtype=jnp.int32)
    proj = attention(order, [early], weights, 64, 1000)
    proj_early = exchange(proj)
    _, *got = lax.optimization_barrier((proj, *got))

    give = jnp.stack([pick(g, other, 1) for g in got]).reshape(FRAMES // 2, share, chans)
    theirs = to_sibling(give)
    slots = []
    for c in (core, other):
        for k in range(4):
            for s in range(2):
                slots.append(((x + c) % 2 * 4 + (y + 4 - k) % 4) * 2 + (c + s) % 2)
    slots = jnp.stack(slots + [core]).astype(jnp.int32)
    proj_late = exchange(attention(slots, [*got, theirs], weights, 64, 5 * 10**9))

    part, last, lead = conv_early(clip, proj_early, w, bias)
    size = lax.axis_size("rows")
    up = lax.ppermute(last, "rows", [(i, i + 1) for i in range(size - 1)])
    down = lax.ppermute(lead, "rows", [(i + 1, i) for i in range(size - 1)])
    return conv_late(clip, proj_late, up, down, part, w, bias)


def solution(mesh):
    placed = (P("frames", "rows", None, None), P(), P(), P(), P(), P(), P())
    return jax.shard_map(
        local,
        mesh=mesh,
        in_specs=placed,
        out_specs=P("frames", "rows", None, None),
        check_vma=False,
    )
```

time: 205 us -> 159 us (0.78)
  blocking collectives: 109 us -> 0 us
  waiting for transfers between devices: 16.4 us -> 51 us
  starting transfers between devices: 8.72 us -> 41.6 us
  Pallas kernels: 62.4 us -> 55 us
  local copies, waits for them, and re-layouts: 3.44 us -> 8.55 us
    all_to_all x2 -> x0, blocking collectives: 109 us -> none  [the longest x1 54.7 us: local(): got = lax.all_to_all(cut, 'frames', split_axis=0, concat_axis=0, tiled=True)]
    all_to_all x0 -> x3, starting transfers between devices: none -> 26.8 us  [exchange(): return lax.all_to_all(a, 'frames', split_axis=0, concat_axis=0, tiled=True)]
    all_to_all x0 -> x3, waiting for transfers between devices: none -> 22.4 us  [exchange(): return lax.all_to_all(a, 'frames', split_axis=0, concat_axis=0, tiled=True)]
    ppermute x2 -> x8, waiting for transfers between devices: 16.4 us -> 28.6 us  [the longest x1 26.7 us: local(): up = lax.ppermute(last, 'rows', [(i, i + 1) for i in range(size - 1)])]
    pallas_call x2 -> x6, Pallas kernels: 62.4 us -> 55 us  [the longest x2 30.6 us: attention(): pl.pallas_call(functools.partial(attention_kernel, len(xs)), out_shape=ja...]
    ppermute x2 -> x8, starting transfers between devices: 8.72 us -> 14.8 us  [the longest x4 6.23 us: to_chip(): return lax.ppermute(a, 'frames', pairs)]
    unnamed x20 -> x10, local copies, waits for them, and re-layouts: 0.84 us -> 3.8 us
    convert_element_type x2 -> x0, other arithmetic: 2.87 us -> none  [the longest x1 2.69 us: edge(): return silu(hidden).astype(BF16)]
  transfers between devices with their start and end apart: 2 -> 11, of which waited for: 2 -> 4; matrix products, arithmetic and copies ran while one was open for 0% -> 4% of each run, Pallas kernels for 0% -> 25%
where the time goes in v1:
time: 159 us; the launch traced here: 158 us
  Pallas kernels  55 us (35%)
  waiting for transfers between devices  51 us (32%)
  starting transfers between devices  41.6 us (26%)
  local copies, waits for them, and re-layouts  8.55 us (5%)
  other arithmetic  1.93 us (1%)
    pallas_call x2, Pallas kernels, attention(): pl.pallas_call(functools.partial(attention_kernel, len(xs)), out_shape=ja...  30.6 us
    all_to_all x3, starting transfers between devices, exchange(): return lax.all_to_all(a, 'frames', split_axis=0, concat_axis=0, tiled=True)  26.8 us
    ppermute x1, waiting for transfers between devices, local(): up = lax.ppermute(last, 'rows', [(i, i + 1) for i in range(size - 1)])  26.7 us
    all_to_all x3, waiting for transfers between devices, exchange(): return lax.all_to_all(a, 'frames', split_axis=0, concat_axis=0, tiled=True)  22.4 us
    pallas_call x1, Pallas kernels, conv_late(): pl.pallas_call(late_kernel, out_shape=out, grid=(frames,), in_specs=[row_...  10.8 us
    pallas_call x1, Pallas kernels, conv_early(): pl.pallas_call(early_kernel, out_shape=outs, grid=(frames,), in_specs=[ro...  8.38 us
    ppermute x4, starting transfers between devices, to_chip(): return lax.ppermute(a, 'frames', pairs)  6.23 us
    ppermute x1, starting transfers between devices, local(): down = lax.ppermute(lead, 'rows', [(i + 1, i) for i in range(size - 1)])  4.37 us
  transfers between devices with their start and end apart: 11, of which 4 were waited for; matrix products, arithmetic and copies ran while one was open for 4% of the time, Pallas kernels for 25%

profile of v1, /device:TPU:10, one launch (start us, length us, event | category | flops | bytes accessed | tf_op | source)
XLA Modules:
  0.0 158.2 jit_solution(1362861379749463342)
XLA Ops:
  0.0 2.6 %early_cut.1 = bf16[4,4,2,128,256]{4,3,2,1,0:T(8,128)(2,1)} custom-call(bf16[2,8,4,128,256]{4,3,2,1,0:T(8,128)(2,1)} %bitcast.35), custom_call_target="tpu_custom_call" | custom-call | flops 1000 | bytes 1000 | tf_op jit(solution)/shard_map/early_cut/pallas_call | solution.py:267
  2.6 2.6 %late_cut.1 = (bf16[2,4,2,128,256]{4,3,2,1,0:T(8,128)(2,1)}, bf16[2,4,2,128,256]{4,3,2,1,0:T(8,128)(2,1)}) custom-call(s32[1]{0:T(128)} %bitcast.20.half_ref, bf16[2,8,4,128,256]{4,3,2,1,0:T(8,128)(2,1)} %bitcast.36, bf16[2,8,4,128,256]{4,3,2,1,0:T(8,128)(2,1)} %bitcast.37), custom_call_target="tpu_custom_call" | custom-call | flops 1000 | bytes 1000 | tf_op jit(solution)/shard_map/late_cut/pallas_call | solution.py:292
  5.2 0.0 collective-permute-start
  5.2 6.6 %all-to-all-start = ((bf16[16,2,128,256]{3,2,1,0:T(8,128)(2,1)}), bf16[16,2,128,256]{3,2,1,0:T(8,128)(2,1)S(1)}, u32[]{:S(2)}, u32[]{:S(2)}) async-start(bf16[16,2,128,256]{3,2,1,0:T(8,128)(2,1)} %bitcast.18), calls=%async_computation | async-start | bytes 4194304 | tf_op jit(solution)/shard_map/all_to_all | solution.py:315
  11.8 1.3 constant_dynamic-slice_fusion.1
  13.1 0.0 collective-permute-done
  13.1 0.1 constant_dynamic-slice_fusion
  13.2 0.1 pad_maximum_fusion.1
  13.3 1.5 collective-permute-start.1
  14.7 0.1 pad_maximum_fusion.2
  14.8 1.5 collective-permute-start.2
  16.3 0.8 pad_maximum_fusion.3
  17.2 0.8 collective-permute-start.3
  18.0 0.8 pad_maximum_fusion.4
  18.8 2.4 %collective-permute-start.4 = (bf16[2,2,2,128,256]{4,3,2,1,0:T(8,128)(2,1)}, bf16[2,2,2,128,256]{4,3,2,1,0:T(8,128)(2,1)}, u32[]{:S(2)}, u32[]{:S(2)}) collective-permute-start(bf16[2,2,2,128,256]{4,3,2,1,0:T(8,128)(2,1)} %pad_maximum_fusion.4), channel_id=1, source_target_pairs={{0,48},{8,120},{16,0},{24,72},{32,16},{40,88},{48,32},{56,104},{64... | collective-permute-start | bytes 1572872 | tf_op jit(solution)/shard_map/ppermute | solution.py:323
  21.2 16.9 %all-to-all-done = bf16[16,2,128,256]{3,2,1,0:T(8,128)(2,1)S(1)} async-done(((bf16[16,2,128,256]{3,2,1,0:T(8,128)(2,1)}), bf16[16,2,128,256]{3,2,1,0:T(8,128)(2,1)S(1)}, u32[]{:S(2)}, u32[]{:S(2)}) %all-to-all-start) | async-done | bytes 2097184 | tf_op jit(solution)/shard_map/all_to_all | solution.py:315
  38.1 0.0 copy-start.1
  38.1 0.6 iota.3.slots_ref
  38.7 0.8 copy-done.1
  39.4 15.2 %attention.2 = bf16[16,2,128,256]{3,2,1,0:T(8,128)(2,1)} custom-call(s32[17]{0:T(128)} %iota.3.slots_ref, bf16[32,128,256]{2,1,0:T(8,128)(2,1)} %bitcast.38, bf16[256,256]{1,0:T(8,128)(2,1)} %refs_5_.2, bf16[256,256]{1,0:T(8,128)(2,1)} %refs_6_.2, bf16[256,256]{1,0:T(8,128)(2,1)} %refs_7_.2, bf16[256,256]{1,0:T(8,128)(2,1)} %refs_8_.1, ...), custom_call_target="tpu_custom_call" | custom-call | flops 1000 | bytes 1 | tf_op jit(solution)/shard_map/attention/pallas_call | solution.py:93
  54.6 11.0 %all-to-all-start.2 = ((bf16[16,2,128,256]{3,2,1,0:T(8,128)(2,1)}), bf16[16,2,128,256]{3,2,1,0:T(8,128)(2,1)S(1)}, u32[]{:S(2)}, u32[]{:S(2)}) async-start(bf16[16,2,128,256]{3,2,1,0:T(8,128)(2,1)} %attention.2), calls=%async_computation.2 | async-start | bytes 4194304 | tf_op jit(solution)/shard_map/all_to_all | solution.py:315
  65.6 0.0 collective-permute-done.1.refs_0_
  65.6 0.0 collective-permute-done.2.refs_1_
  65.6 0.0 collective-permute-done.3.refs_2_
  65.6 0.0 collective-permute-done.4.refs_3_
  65.6 1.1 dynamic-slice_bitcast_fusion.2
  66.7 1.1 dynamic-slice_bitcast_fusion
  67.8 0.1 pad_maximum_fusion
  67.9 0.4 collective-permute-start.5
  68.4 0.7 stack.106.slots_ref
  69.0 2.0 %collective-permute-done.5.refs_4_ = bf16[16,128,256]{2,1,0:T(8,128)(2,1)} collective-permute-done((bf16[16,128,256]{2,1,0:T(8,128)(2,1)S(1)}, bf16[16,128,256]{2,1,0:T(8,128)(2,1)}, u32[]{:S(2)}, u32[]{:S(2)}) %collective-permute-start.5) | collective-permute-done | bytes 1048608 | tf_op jit(solution)/shard_map/ppermute | solution.py:327
  71.0 15.4 %attention.3 = bf16[16,2,128,256]{3,2,1,0:T(8,128)(2,1)} custom-call(s32[17]{0:T(128)} %stack.106.slots_ref, bf16[2,2,2,128,256]{4,3,2,1,0:T(8,128)(2,1)} %collective-permute-done.1.refs_0_, bf16[2,2,2,128,256]{4,3,2,1,0:T(8,128)(2,1)} %collective-permute-done.2.refs_1_, bf16[2,2,2,128,256]{4,3,2,1,0:T(8,128)(2,1)} %collective-permute-done.3.refs_2_, ...), custom_call_target="tpu_custom_call" | custom-call | flops 5000000000 | bytes 5000000 | tf_op jit(solution)/shard_map/attention/pallas_call | solution.py:93
  86.4 5.5 %all-to-all-done.2.proj_ref = bf16[16,2,128,256]{3,2,1,0:T(8,128)(2,1)S(1)} async-done(((bf16[16,2,128,256]{3,2,1,0:T(8,128)(2,1)}), bf16[16,2,128,256]{3,2,1,0:T(8,128)(2,1)S(1)}, u32[]{:S(2)}, u32[]{:S(2)}) %all-to-all-start.2) | async-done | bytes 2097184 | tf_op jit(solution)/shard_map/all_to_all | solution.py:315
  91.9 0.0 copy-start.2
  91.9 1.4 copy-done.2
  93.2 9.2 %all-to-all-start.1 = ((bf16[16,2,128,256]{3,2,1,0:T(8,128)(2,1)}), bf16[16,2,128,256]{3,2,1,0:T(8,128)(2,1)S(1)}, u32[]{:S(2)}, u32[]{:S(2)}) async-start(bf16[16,2,128,256]{3,2,1,0:T(8,128)(2,1)} %attention.3), calls=%async_computation.1 | async-start | bytes 4194304 | tf_op jit(solution)/shard_map/all_to_all | solution.py:315
  102.5 8.4 %conv_early.1 = (f32[2,6,512,256]{3,2,1,0:T(8,128)}, bf16[2,1,512,256]{3,2,1,0:T(8,128)(2,1)}, bf16[2,1,512,256]{3,2,1,0:T(8,128)(2,1)}) custom-call(bf16[2,8,512,256]{3,2,1,0:T(8,128)(2,1)} %bottom_ref.3, bf16[2,8,512,256]{3,2,1,0:T(8,128)(2,1)} %bottom_ref.3, bf16[16,2,128,256]{3,2,1,0:T(8,128)(2,1)} %copy-done.2, bf16[3,768,256]{2,1,0:T(8,128)(2,1)} %bitcast.39, ...), custom_call_target="tpu_custom_call" | custom-call | flops 4831838208 | bytes 8388608 | tf_op jit(solution)/shard_map/conv_early/pallas_call | solution.py:219
  110.9 3.8 %collective-permute-start.6 = (bf16[2,1,512,256]{3,2,1,0:T(8,128)(2,1)}, bf16[2,1,512,256]{3,2,1,0:T(8,128)(2,1)S(1)}, u32[]{:S(2)}, u32[]{:S(2)}) collective-permute-start(bf16[2,1,512,256]{3,2,1,0:T(8,128)(2,1)} %get-tuple-element.24), channel_id=1, source_target_pairs={{0,1},{1,2},{2,3},{3,4},{4,5},{5,6},{6,7},{8,9},{9,10},{10,11},{11... | collective-permute-start | bytes 1572872 | tf_op jit(solution)/shard_map/ppermute | solution.py:372
  114.7 4.4 %collective-permute-start.7 = (bf16[2,1,512,256]{3,2,1,0:T(8,128)(2,1)}, bf16[2,1,512,256]{3,2,1,0:T(8,128)(2,1)S(1)}, u32[]{:S(2)}, u32[]{:S(2)}) collective-permute-start(bf16[2,1,512,256]{3,2,1,0:T(8,128)(2,1)} %get-tuple-element.25), channel_id=1, source_target_pairs={{1,0},{2,1},{3,2},{4,3},{5,4},{6,5},{7,6},{9,8},{10,9},{11,10},{12... | collective-permute-start | bytes 1572872 | tf_op jit(solution)/shard_map/ppermute | solution.py:373
  119.1 26.7 %collective-permute-done.6.up_ref = bf16[2,1,512,256]{3,2,1,0:T(8,128)(2,1)S(1)} collective-permute-done((bf16[2,1,512,256]{3,2,1,0:T(8,128)(2,1)}, bf16[2,1,512,256]{3,2,1,0:T(8,128)(2,1)S(1)}, u32[]{:S(2)}, u32[]{:S(2)}) %collective-permute-start.6) | collective-permute-done | bytes 524320 | tf_op jit(solution)/shard_map/ppermute | solution.py:372
  145.7 0.0 copy-start.3
  145.7 0.0 collective-permute-done.7.down_ref
  145.7 0.0 copy-start.4
  145.7 0.0 all-to-all-done.1.proj_ref
  145.7 0.0 copy-start
  145.8 0.8 copy-done.3
  146.5 0.3 copy-done.4
  146.8 0.6 copy-done
  147.4 10.8 %conv_late.1 = bf16[2,16,512,128]{3,2,1,0:T(8,128)(2,1)} custom-call(bf16[2,8,512,256]{3,2,1,0:T(8,128)(2,1)} %bottom_ref.3, bf16[2,8,512,256]{3,2,1,0:T(8,128)(2,1)} %bottom_ref.3, bf16[16,2,128,256]{3,2,1,0:T(8,128)(2,1)} %copy-done, bf16[2,1,512,256]{3,2,1,0:T(8,128)(2,1)} %copy-done.3, bf16[2,1,512,256]{3,2,1,0:T(8,128)(2,1)} %copy-done.4, ...), custom_call_target="tpu_custom_call" | custom-call | flops 4831838208 | bytes 8388608 | tf_op jit(solution)/shard_map/conv_late/pallas_call | solution.py:236
Async XLA Ops:
  5.2 7.9 %collective-permute-start = (bf16[4,2,2,128,256]{4,3,2,1,0:T(8,128)(2,1)}, bf16[4,2,2,128,256]{4,3,2,1,0:T(8,128)(2,1)S(1)}, u32[]{:S(2)}, u32[]{:S(2)}) collective-permute-start(bf16[4,2,2,128,256]{4,3,2,1,0:T(8,128)(2,1)} %bitcast.45), channel_id=1, source_target_pairs={{0,8},{8,0},{16,24},{24,16},{32,40},{40,32},{48,56},{56,48},{64,72... | collective-permute-start | bytes 3145736 | tf_op jit(solution)/shard_map/ppermute | solution.py:327
  5.2 32.9 %all-to-all-start = ((bf16[16,2,128,256]{3,2,1,0:T(8,128)(2,1)}), bf16[16,2,128,256]{3,2,1,0:T(8,128)(2,1)S(1)}, u32[]{:S(2)}, u32[]{:S(2)}) async-start(bf16[16,2,128,256]{3,2,1,0:T(8,128)(2,1)} %bitcast.18), calls=%async_computation | async-start | bytes 4194304 | tf_op jit(solution)/shard_map/all_to_all | solution.py:315
  13.3 52.3 %collective-permute-start.1 = (bf16[2,2,2,128,256]{4,3,2,1,0:T(8,128)(2,1)S(1)}, bf16[2,2,2,128,256]{4,3,2,1,0:T(8,128)(2,1)}, u32[]{:S(2)}, u32[]{:S(2)}) collective-permute-start(bf16[2,2,2,128,256]{4,3,2,1,0:T(8,128)(2,1)S(1)} %pad_maximum_fusion.1), channel_id=1, source_target_pairs={{0,0},{8,72},{16,16},{24,88},{32,32},{40,104},{48,48},{56,120},{64... | collective-permute-start | bytes 1572872 | tf_op jit(solution)/shard_map/ppermute | solution.py:323
  14.8 50.8 %collective-permute-start.2 = (bf16[2,2,2,128,256]{4,3,2,1,0:T(8,128)(2,1)S(1)}, bf16[2,2,2,128,256]{4,3,2,1,0:T(8,128)(2,1)}, u32[]{:S(2)}, u32[]{:S(2)}) collective-permute-start(bf16[2,2,2,128,256]{4,3,2,1,0:T(8,128)(2,1)S(1)} %pad_maximum_fusion.2), channel_id=1, source_target_pairs={{0,16},{8,88},{16,32},{24,104},{32,48},{40,120},{48,0},{56,72},{64... | collective-permute-start | bytes 1572872 | tf_op jit(solution)/shard_map/ppermute | solution.py:323
  17.2 48.5 %collective-permute-start.3 = (bf16[2,2,2,128,256]{4,3,2,1,0:T(8,128)(2,1)}, bf16[2,2,2,128,256]{4,3,2,1,0:T(8,128)(2,1)}, u32[]{:S(2)}, u32[]{:S(2)}) collective-permute-start(bf16[2,2,2,128,256]{4,3,2,1,0:T(8,128)(2,1)} %pad_maximum_fusion.3), channel_id=1, source_target_pairs={{0,32},{8,104},{16,48},{24,120},{32,0},{40,72},{48,16},{56,88},{64... | collective-permute-start | bytes 1572872 | tf_op jit(solution)/shard_map/ppermute | solution.py:323
  18.8 46.8 %collective-permute-start.4 = (bf16[2,2,2,128,256]{4,3,2,1,0:T(8,128)(2,1)}, bf16[2,2,2,128,256]{4,3,2,1,0:T(8,128)(2,1)}, u32[]{:S(2)}, u32[]{:S(2)}) collective-permute-start(bf16[2,2,2,128,256]{4,3,2,1,0:T(8,128)(2,1)} %pad_maximum_fusion.4), channel_id=1, source_target_pairs={{0,48},{8,120},{16,0},{24,72},{32,16},{40,88},{48,32},{56,104},{64... | collective-permute-start | bytes 1572872 | tf_op jit(solution)/shard_map/ppermute | solution.py:323
  38.1 1.3 copy-start.1
  54.6 37.2 %all-to-all-start.2 = ((bf16[16,2,128,256]{3,2,1,0:T(8,128)(2,1)}), bf16[16,2,128,256]{3,2,1,0:T(8,128)(2,1)S(1)}, u32[]{:S(2)}, u32[]{:S(2)}) async-start(bf16[16,2,128,256]{3,2,1,0:T(8,128)(2,1)} %attention.2), calls=%async_computation.2 | async-start | bytes 4194304 | tf_op jit(solution)/shard_map/all_to_all | solution.py:315
  67.9 3.1 %collective-permute-start.5 = (bf16[16,128,256]{2,1,0:T(8,128)(2,1)S(1)}, bf16[16,128,256]{2,1,0:T(8,128)(2,1)}, u32[]{:S(2)}, u32[]{:S(2)}) collective-permute-start(bf16[16,128,256]{2,1,0:T(8,128)(2,1)S(1)} %bitcast.42), channel_id=1, source_target_pairs={{0,8},{8,0},{16,24},{24,16},{32,40},{40,32},{48,56},{56,48},{64,72... | collective-permute-start | bytes 3145736 | tf_op jit(solution)/shard_map/ppermute | solution.py:327
  91.9 1.4 copy-start.2
  93.2 52.5 %all-to-all-start.1 = ((bf16[16,2,128,256]{3,2,1,0:T(8,128)(2,1)}), bf16[16,2,128,256]{3,2,1,0:T(8,128)(2,1)S(1)}, u32[]{:S(2)}, u32[]{:S(2)}) async-start(bf16[16,2,128,256]{3,2,1,0:T(8,128)(2,1)} %attention.3), calls=%async_computation.1 | async-start | bytes 4194304 | tf_op jit(solution)/shard_map/all_to_all | solution.py:315
  110.9 34.9 %collective-permute-start.6 = (bf16[2,1,512,256]{3,2,1,0:T(8,128)(2,1)}, bf16[2,1,512,256]{3,2,1,0:T(8,128)(2,1)S(1)}, u32[]{:S(2)}, u32[]{:S(2)}) collective-permute-start(bf16[2,1,512,256]{3,2,1,0:T(8,128)(2,1)} %get-tuple-element.24), channel_id=1, source_target_pairs={{0,1},{1,2},{2,3},{3,4},{4,5},{5,6},{6,7},{8,9},{9,10},{10,11},{11... | collective-permute-start | bytes 1572872 | tf_op jit(solution)/shard_map/ppermute | solution.py:372
  114.7 31.1 %collective-permute-start.7 = (bf16[2,1,512,256]{3,2,1,0:T(8,128)(2,1)}, bf16[2,1,512,256]{3,2,1,0:T(8,128)(2,1)S(1)}, u32[]{:S(2)}, u32[]{:S(2)}) collective-permute-start(bf16[2,1,512,256]{3,2,1,0:T(8,128)(2,1)} %get-tuple-element.25), channel_id=1, source_target_pairs={{1,0},{2,1},{3,2},{4,3},{5,4},{6,5},{7,6},{9,8},{10,9},{11,10},{12... | collective-permute-start | bytes 1572872 | tf_op jit(solution)/shard_map/ppermute | solution.py:373
  145.7 0.8 copy-start.3
  145.7 1.1 copy-start.4
  145.7 1.7 %copy-start = (bf16[16,2,128,256]{3,2,1,0:T(8,128)(2,1)}, bf16[16,2,128,256]{3,2,1,0:T(8,128)(2,1)S(1)}, u32[]{:S(2)}) copy-start(bf16[16,2,128,256]{3,2,1,0:T(8,128)(2,1)S(1)} %all-to-all-done.1.proj_ref) | copy-start | bytes 6291460

commit v2 on v1

--- a/solution.py
+++ b/solution.py
@@ -13,7 +13,7 @@
 FRAMES = 32
 C = 256
 GROUP = 8
-VMEM = 60 * 2**20
+VMEM = 63 * 2**20
 F32 = jnp.float32
 BF16 = jnp.bfloat16
 
@@ -33,7 +33,8 @@
     return jnp.broadcast_to(m, (HEADS, HEAD, rows)).reshape(C, rows).T
 
 
-def attention_kernel(parts_in, slots_ref, *refs):
+def attention_kernel(parts_in, ordered, *refs):
+    slots_ref, refs = (range(FRAMES // 2), refs) if ordered else (refs[0], refs[1:])
     x_refs = refs[:parts_in]
     wq_ref, wk_ref, wv_ref, wo_ref, perm_ref, back_ref, same_ref = refs[parts_in : parts_in + 7]
     out_ref = refs[-1]
@@ -76,33 +77,34 @@
 
 
 def attention(slots, xs, weights, pixels, cost):
+    slots = [] if slots is None else [slots]
     count = xs[0].shape[-2]
     row = np.arange(GROUP * FRAMES)
     source = (row % FRAMES) * GROUP + row // FRAMES
     perm = (source[:, None] == row[None, :]).astype(np.float32)
     same = (row[:, None] // HEAD == row[None, :] // HEAD).astype(np.float32)
-    whole = pl.BlockSpec((C, C), lambda i, s: (0, 0))
+    whole = pl.BlockSpec((C, C), lambda i, *s: (0, 0))
     blocks = []
     for x in xs:
         if x.ndim == 3:
-            blocks.append(pl.BlockSpec((x.shape[0], pixels, C), lambda i, s: (0, i, 0)))
+            blocks.append(pl.BlockSpec((x.shape[0], pixels, C), lambda i, *s: (0, i, 0)))
         else:
             shape = (x.shape[0], 1, x.shape[2], pixels, C)
             blocks.append(pl.BlockSpec(shape, lambda i, s: (0, s[FRAMES // 2], 0, i, 0)))
     pairs = FRAMES // 2
     return pl.pallas_call(
-        functools.partial(attention_kernel, len(xs)),
+        functools.partial(attention_kernel, len(xs), not slots),
         out_shape=jax.ShapeDtypeStruct((pairs, 2, count, C), BF16),
         grid_spec=pltpu.PrefetchScalarGridSpec(
-            num_scalar_prefetch=1,
+            num_scalar_prefetch=len(slots),
             grid=(count // pixels,),
             in_specs=blocks + [whole] * 7,
-            out_specs=pl.BlockSpec((pairs, 2, pixels, C), lambda i, s: (0, 0, i, 0)),
+            out_specs=pl.BlockSpec((pairs, 2, pixels, C), lambda i, *s: (0, 0, i, 0)),
         ),
         compiler_params=pltpu.CompilerParams(vmem_limit_bytes=VMEM),
         cost_estimate=pl.CostEstimate(flops=cost, bytes_accessed=cost // 1000, transcendentals=0),
         name="attention",
-    )(slots, *xs, *weights, jnp.asarray(perm, BF16), jnp.asarray(perm.T, BF16), jnp.asarray(same, BF16))
+    )(*slots, *xs, *weights, jnp.asarray(perm, BF16), jnp.asarray(perm.T, BF16), jnp.asarray(same, BF16))
 
 
 def silu(v):
@@ -276,36 +278,29 @@
     )(clip.reshape(frames, rows, runs, share, C)).reshape(owners, frames, share, C)
 
 
-def late_cut_kernel(half_ref, near_ref, far_ref, mine_ref, away_ref):
-    mine_ref[:, :, 0] = near_ref[0]
-    away_ref[:, :, 0] = far_ref[0]
+def late_cut_kernel(half_ref, clip_ref, out_ref):
+    for f in range(out_ref.shape[2]):
+        out_ref[:, :, f] = clip_ref[f]
 
 
 def late_cut(half, clip, owners):
     frames, rows, width, _ = clip.shape
     share = 4 * width // owners
     runs = width // share
-    out = jax.ShapeDtypeStruct((2, runs, frames, share, C), BF16)
-    block = (1, 2, runs, share, C)
-    out_spec = pl.BlockSpec((2, runs, 1, share, C), lambda f, s: (0, 0, f, 0, 0))
-    clip = clip.reshape(frames, rows, runs, share, C)
-    outs = pl.pallas_call(
+    out = pl.pallas_call(
         late_cut_kernel,
-        out_shape=(out, out),
+        out_shape=jax.ShapeDtypeStruct((2, runs, frames, share, C), BF16),
         grid_spec=pltpu.PrefetchScalarGridSpec(
             num_scalar_prefetch=1,
-            grid=(frames,),
-            in_specs=[
-                pl.BlockSpec(block, lambda f, s: (f, LATE[0] + s[0], 0, 0, 0)),
-                pl.BlockSpec(block, lambda f, s: (f, LATE[1] - s[0], 0, 0, 0)),
-            ],
-            out_specs=(out_spec, out_spec),
+            grid=(1,),
+            in_specs=[pl.BlockSpec((frames, 2, runs, share, C), lambda i, s: (0, LATE[0] + s[0], 0, 0, 0))],
+            out_specs=pl.BlockSpec((2, runs, frames, share, C), lambda i, s: (0, 0, 0, 0, 0)),
         ),
         compiler_params=pltpu.CompilerParams(vmem_limit_bytes=VMEM),
         cost_estimate=pl.CostEstimate(flops=1000, bytes_accessed=1000, transcendentals=0),
         name="late_cut",
-    )(half, clip, clip)
-    return [o.reshape(owners // 4, 2, frames, share, C) for o in outs]
+    )(half, clip.reshape(frames, rows, runs, share, C))
+    return out.reshape(owners // 4, 2, frames, share, C)
 
 
 CHIPS = 8
@@ -345,15 +340,15 @@
     share = early.shape[2]
     early = early.reshape(FRAMES, share, chans)
 
-    mine, away = late_cut(((x + core) % 2).astype(jnp.int32).reshape(1), clip_late, 2 * CHIPS)
-    theirs = to_sibling(away)
+    theirs = to_sibling(late_cut((x + other).astype(jnp.int32).reshape(1) % 2, clip_late, 2 * CHIPS))
+    clip_late, theirs = lax.optimization_barrier((clip_late, theirs))
+    mine = late_cut((x + core).astype(jnp.int32).reshape(1) % 2, clip_late, 2 * CHIPS)
     got = []
     for k in range(4):
         to = (y + k) % 4
         got.append(to_chip(jnp.stack([pick(mine, to), pick(theirs, to)]), k))
 
-    order = jnp.arange(2 * CHIPS + 1, dtype=jnp.int32)
-    proj = attention(order, [early], weights, 64, 1000)
+    proj = attention(None, [early], weights, 64, 1000)
     proj_early = exchange(proj)
     _, *got = lax.optimization_barrier((proj, *got))
 

time: 159 us -> 154 us (0.969)
  waiting for transfers between devices: 51 us -> 45 us
    all_to_all x3, waiting for transfers between devices: 22.4 us -> 17.7 us  [exchange(): return lax.all_to_all(a, 'frames', split_axis=0, concat_axis=0, tiled=True)]
    unnamed x10 -> x2, local copies, waits for them, and re-layouts: 3.8 us -> 0.78 us
    another operation x2 -> x4, local copies, waits for them, and re-layouts: 2.15 us -> 3.91 us  [local(): jnp.stack([pick(g, other, 1) for g in got])]
    pallas_call x3 -> x4, Pallas kernels: 33.2 us -> 34.4 us  [the longest x2 29.9 us: attention(): pl.pallas_call(functools.partial(attention_kernel, len(xs), not slots), o...]
  transfers between devices with their start and end apart: 11 -> 11, of which waited for: 4 -> 4; matrix products, arithmetic and copies ran while one was open for 4% -> 6% of each run, Pallas kernels for 25% -> 27%
where the time goes in v2:
time: 154 us; the launch traced here: 153 us
  Pallas kernels  56.2 us (36%)
  waiting for transfers between devices  45 us (29%)
  starting transfers between devices  41.8 us (27%)
  local copies, waits for them, and re-layouts  7.02 us (5%)
  other arithmetic  2.78 us (2%)
    pallas_call x2, Pallas kernels, attention(): pl.pallas_call(functools.partial(attention_kernel, len(xs), not slots), o...  29.9 us
    all_to_all x3, starting transfers between devices, exchange(): return lax.all_to_all(a, 'frames', split_axis=0, concat_axis=0, tiled=True)  27 us
    ppermute x1, waiting for transfers between devices, local(): up = lax.ppermute(last, 'rows', [(i, i + 1) for i in range(size - 1)])  25.6 us
    all_to_all x3, waiting for transfers between devices, exchange(): return lax.all_to_all(a, 'frames', split_axis=0, concat_axis=0, tiled=True)  17.7 us
    pallas_call x1, Pallas kernels, conv_late(): pl.pallas_call(late_kernel, out_shape=out, grid=(frames,), in_specs=[row_...  10.8 us
    pallas_call x1, Pallas kernels, conv_early(): pl.pallas_call(early_kernel, out_shape=outs, grid=(frames,), in_specs=[ro...  8.37 us
    ppermute x4, starting transfers between devices, to_chip(): return lax.ppermute(a, 'frames', pairs)  6.16 us
    pallas_call x2, Pallas kernels, late_cut(): pl.pallas_call(late_cut_kernel, out_shape=jax.ShapeDtypeStruct((2, runs,...  4.57 us
  transfers between devices with their start and end apart: 11, of which 4 were waited for; matrix products, arithmetic and copies ran while one was open for 6% of the time, Pallas kernels for 27%

profile of v2, /device:TPU:10, one launch (start us, length us, event | category | flops | bytes accessed | tf_op | source)
XLA Modules:
  0.0 152.9 jit_solution(13932724810637987546)
XLA Ops:
  0.0 2.6 %early_cut.1 = bf16[4,4,2,128,256]{4,3,2,1,0:T(8,128)(2,1)} custom-call(bf16[2,8,4,128,256]{4,3,2,1,0:T(8,128)(2,1)} %bitcast.37), custom_call_target="tpu_custom_call" | custom-call | flops 1000 | bytes 1000 | tf_op jit(solution)/shard_map/early_cut/pallas_call | solution.py:269
  2.6 2.3 %late_cut.2 = bf16[2,4,2,128,256]{4,3,2,1,0:T(8,128)(2,1)} custom-call(s32[1]{0:T(128)S(6)} %select_n.193.half_ref, bf16[2,8,4,128,256]{4,3,2,1,0:T(8,128)(2,1)} %bitcast.38), custom_call_target="tpu_custom_call" | custom-call | flops 1000 | bytes 1000 | tf_op jit(solution)/shard_map/late_cut/pallas_call | solution.py:290
  4.9 0.0 collective-permute-start
  4.9 6.6 %all-to-all-start = ((bf16[16,2,128,256]{3,2,1,0:T(8,128)(2,1)}), bf16[16,2,128,256]{3,2,1,0:T(8,128)(2,1)}, u32[]{:S(2)}, u32[]{:S(2)}) async-start(bf16[16,2,128,256]{3,2,1,0:T(8,128)(2,1)} %bitcast.40), calls=%async_computation | async-start | bytes 4194304 | tf_op jit(solution)/shard_map/all_to_all | solution.py:310
  11.5 0.0 collective-permute-done
  11.5 2.3 %late_cut.3 = bf16[2,4,2,128,256]{4,3,2,1,0:T(8,128)(2,1)} custom-call(s32[1]{0:T(128)S(6)} %select_n.192.half_ref, bf16[2,8,4,128,256]{4,3,2,1,0:T(8,128)(2,1)} %bitcast.39), custom_call_target="tpu_custom_call" | custom-call | flops 1000 | bytes 1000 | tf_op jit(solution)/shard_map/late_cut/pallas_call | solution.py:290
  13.8 1.6 %constant_dynamic-slice_fusion = (bf16[1,2,2,128,256]{4,3,2,1,0:T(8,128)(2,1)S(1)}, bf16[1,2,2,128,256]{4,3,2,1,0:T(8,128)(2,1)S(1)}, bf16[1,2,2,128,256]{4,3,2,...) fusion(bf16[4,2,2,128,256]{4,3,2,1,0:T(8,128)(2,1)} %collective, ...), kind=kLoop, calls=%fused_computation.9 | loop fusion | bytes 4194320 | tf_op jit(solution)/shard_map/jit(dynamic_index_in_dim)/dynamic_slice | solution.py:326
  15.4 0.1 pad_maximum_fusion.1
  15.5 1.5 collective-permute-start.1
  17.0 0.9 pad_maximum_fusion.2
  17.8 1.5 collective-permute-start.2
  19.3 0.9 pad_maximum_fusion.3
  20.2 0.9 collective-permute-start.3
  21.1 0.9 pad_maximum_fusion.4
  21.9 2.4 %collective-permute-start.4 = (bf16[2,2,2,128,256]{4,3,2,1,0:T(8,128)(2,1)}, bf16[2,2,2,128,256]{4,3,2,1,0:T(8,128)(2,1)}, u32[]{:S(2)}, u32[]{:S(2)}) collective-permute-start(bf16[2,2,2,128,256]{4,3,2,1,0:T(8,128)(2,1)} %pad_maximum_fusion.4), channel_id=1, source_target_pairs={{0,48},{8,120},{16,0},{24,72},{32,16},{40,88},{48,32},{56,104},{64... | collective-permute-start | bytes 1572872 | tf_op jit(solution)/shard_map/ppermute | solution.py:318
  24.3 13.6 %all-to-all-done = bf16[16,2,128,256]{3,2,1,0:T(8,128)(2,1)} async-done(((bf16[16,2,128,256]{3,2,1,0:T(8,128)(2,1)}), bf16[16,2,128,256]{3,2,1,0:T(8,128)(2,1)}, u32[]{:S(2)}, u32[]{:S(2)}) %all-to-all-start) | async-done | bytes 2097184 | tf_op jit(solution)/shard_map/all_to_all | solution.py:310
  37.9 14.5 %attention.2 = bf16[16,2,128,256]{3,2,1,0:T(8,128)(2,1)} custom-call(bf16[32,128,256]{2,1,0:T(8,128)(2,1)} %bitcast.19.refs_0_, bf16[256,256]{1,0:T(8,128)(2,1)} %refs_6_.2, bf16[256,256]{1,0:T(8,128)(2,1)} %refs_7_.2, bf16[256,256]{1,0:T(8,128)(2,1)} %refs_8_.1, bf16[256,256]{1,0:T(8,128)(2,1)} %refs_9_.1, ...), custom_call_target="tpu_custom_call" | custom-call | flops 1000 | bytes 1 | tf_op jit(solution)/shard_map/attention/pallas_call | solution.py:95
  52.4 11.0 %all-to-all-start.2 = ((bf16[16,2,128,256]{3,2,1,0:T(8,128)(2,1)}), bf16[16,2,128,256]{3,2,1,0:T(8,128)(2,1)}, u32[]{:S(2)}, u32[]{:S(2)}) async-start(bf16[16,2,128,256]{3,2,1,0:T(8,128)(2,1)} %attention.2), calls=%async_computation.2 | async-start | bytes 4194304 | tf_op jit(solution)/shard_map/all_to_all | solution.py:310
  63.3 0.0 collective-permute-done.1.refs_1_
  63.3 0.0 collective-permute-done.2.refs_2_
  63.4 0.0 collective-permute-done.3.refs_3_
  63.4 0.0 collective-permute-done.4.refs_4_
  63.4 1.0 dynamic-slice_bitcast_fusion.3
  64.4 1.0 dynamic-slice_bitcast_fusion.2
  65.3 1.0 dynamic-slice_bitcast_fusion.1
  66.3 1.0 dynamic-slice_bitcast_fusion
  67.3 0.1 pad_maximum_fusion
  67.4 0.7 collective-permute-start.5
  68.1 0.7 stack.106.refs_0_
  68.8 1.7 %collective-permute-done.5.refs_5_ = bf16[16,128,256]{2,1,0:T(8,128)(2,1)} collective-permute-done((bf16[16,128,256]{2,1,0:T(8,128)(2,1)S(1)}, bf16[16,128,256]{2,1,0:T(8,128)(2,1)}, u32[]{:S(2)}, u32[]{:S(2)}) %collective-permute-start.5) | collective-permute-done | bytes 1048608 | tf_op jit(solution)/shard_map/ppermute | solution.py:322
  70.6 15.4 %attention.3 = bf16[16,2,128,256]{3,2,1,0:T(8,128)(2,1)} custom-call(s32[17]{0:T(128)} %stack.106.refs_0_, bf16[2,2,2,128,256]{4,3,2,1,0:T(8,128)(2,1)} %collective-permute-done.1.refs_1_, bf16[2,2,2,128,256]{4,3,2,1,0:T(8,128)(2,1)} %collective-permute-done.2.refs_2_, bf16[2,2,2,128,256]{4,3,2,1,0:T(8,128)(2,1)} %collective-permute-done.3.refs_3_, ...), custom_call_target="tpu_custom_call" | custom-call | flops 5000000000 | bytes 5000000 | tf_op jit(solution)/shard_map/attention/pallas_call | solution.py:95
  85.9 4.1 %all-to-all-done.2.proj_ref = bf16[16,2,128,256]{3,2,1,0:T(8,128)(2,1)} async-done(((bf16[16,2,128,256]{3,2,1,0:T(8,128)(2,1)}), bf16[16,2,128,256]{3,2,1,0:T(8,128)(2,1)}, u32[]{:S(2)}, u32[]{:S(2)}) %all-to-all-start.2) | async-done | bytes 2097184 | tf_op jit(solution)/shard_map/all_to_all | solution.py:310
  90.0 9.4 %all-to-all-start.1 = ((bf16[16,2,128,256]{3,2,1,0:T(8,128)(2,1)}), bf16[16,2,128,256]{3,2,1,0:T(8,128)(2,1)}, u32[]{:S(2)}, u32[]{:S(2)}) async-start(bf16[16,2,128,256]{3,2,1,0:T(8,128)(2,1)} %attention.3), calls=%async_computation.1 | async-start | bytes 4194304 | tf_op jit(solution)/shard_map/all_to_all | solution.py:310
  99.4 8.4 %conv_early.1 = (f32[2,6,512,256]{3,2,1,0:T(8,128)}, bf16[2,1,512,256]{3,2,1,0:T(8,128)(2,1)}, bf16[2,1,512,256]{3,2,1,0:T(8,128)(2,1)}) custom-call(bf16[2,8,512,256]{3,2,1,0:T(8,128)(2,1)} %bottom_ref.3, bf16[2,8,512,256]{3,2,1,0:T(8,128)(2,1)} %bottom_ref.3, bf16[16,2,128,256]{3,2,1,0:T(8,128)(2,1)} %all-to-all-done.2.proj_ref, ...), custom_call_target="tpu_custom_call" | custom-call | flops 4831838208 | bytes 8388608 | tf_op jit(solution)/shard_map/conv_early/pallas_call | solution.py:221
  107.8 3.8 %collective-permute-start.6 = (bf16[2,1,512,256]{3,2,1,0:T(8,128)(2,1)}, bf16[2,1,512,256]{3,2,1,0:T(8,128)(2,1)S(1)}, u32[]{:S(2)}, u32[]{:S(2)}) collective-permute-start(bf16[2,1,512,256]{3,2,1,0:T(8,128)(2,1)} %get-tuple-element.24), channel_id=1, source_target_pairs={{0,1},{1,2},{2,3},{3,4},{4,5},{5,6},{6,7},{8,9},{9,10},{10,11},{11... | collective-permute-start | bytes 1572872 | tf_op jit(solution)/shard_map/ppermute | solution.py:367
  111.6 4.1 %collective-permute-start.7 = (bf16[2,1,512,256]{3,2,1,0:T(8,128)(2,1)}, bf16[2,1,512,256]{3,2,1,0:T(8,128)(2,1)}, u32[]{:S(2)}, u32[]{:S(2)}) collective-permute-start(bf16[2,1,512,256]{3,2,1,0:T(8,128)(2,1)} %get-tuple-element.25), channel_id=1, source_target_pairs={{1,0},{2,1},{3,2},{4,3},{5,4},{6,5},{7,6},{9,8},{10,9},{11,10},{12... | collective-permute-start | bytes 1572872 | tf_op jit(solution)/shard_map/ppermute | solution.py:368
  115.8 25.6 %collective-permute-done.6.up_ref = bf16[2,1,512,256]{3,2,1,0:T(8,128)(2,1)S(1)} collective-permute-done((bf16[2,1,512,256]{3,2,1,0:T(8,128)(2,1)}, bf16[2,1,512,256]{3,2,1,0:T(8,128)(2,1)S(1)}, u32[]{:S(2)}, u32[]{:S(2)}) %collective-permute-start.6) | collective-permute-done | bytes 524320 | tf_op jit(solution)/shard_map/ppermute | solution.py:367
  141.4 0.0 copy-start
  141.4 0.0 collective-permute-done.7.down_ref
  141.4 0.0 all-to-all-done.1.proj_ref
  141.4 0.8 copy-done
  142.1 10.8 %conv_late.1 = bf16[2,16,512,128]{3,2,1,0:T(8,128)(2,1)} custom-call(bf16[2,8,512,256]{3,2,1,0:T(8,128)(2,1)} %bottom_ref.3, bf16[2,8,512,256]{3,2,1,0:T(8,128)(2,1)} %bottom_ref.3, bf16[16,2,128,256]{3,2,1,0:T(8,128)(2,1)} %all-to-all-done.1.proj_ref, bf16[2,1,512,256]{3,2,1,0:T(8,128)(2,1)} %copy-done, ...), custom_call_target="tpu_custom_call" | custom-call | flops 4831838208 | bytes 8388608 | tf_op jit(solution)/shard_map/conv_late/pallas_call | solution.py:238
Async XLA Ops:
  4.9 6.6 %collective-permute-start = (bf16[4,2,2,128,256]{4,3,2,1,0:T(8,128)(2,1)}, bf16[4,2,2,128,256]{4,3,2,1,0:T(8,128)(2,1)}, u32[]{:S(2)}, u32[]{:S(2)}) collective-permute-start(bf16[4,2,2,128,256]{4,3,2,1,0:T(8,128)(2,1)} %bitcast.45), channel_id=1, source_target_pairs={{0,8},{8,0},{16,24},{24,16},{32,40},{40,32},{48,56},{56,48},{64,72... | collective-permute-start | bytes 3145736 | tf_op jit(solution)/shard_map/ppermute | solution.py:322
  4.9 33.0 %all-to-all-start = ((bf16[16,2,128,256]{3,2,1,0:T(8,128)(2,1)}), bf16[16,2,128,256]{3,2,1,0:T(8,128)(2,1)}, u32[]{:S(2)}, u32[]{:S(2)}) async-start(bf16[16,2,128,256]{3,2,1,0:T(8,128)(2,1)} %bitcast.40), calls=%async_computation | async-start | bytes 4194304 | tf_op jit(solution)/shard_map/all_to_all | solution.py:310
  15.5 47.8 %collective-permute-start.1 = (bf16[2,2,2,128,256]{4,3,2,1,0:T(8,128)(2,1)S(1)}, bf16[2,2,2,128,256]{4,3,2,1,0:T(8,128)(2,1)}, u32[]{:S(2)}, u32[]{:S(2)}) collective-permute-start(bf16[2,2,2,128,256]{4,3,2,1,0:T(8,128)(2,1)S(1)} %pad_maximum_fusion.1), channel_id=1, source_target_pairs={{0,0},{8,72},{16,16},{24,88},{32,32},{40,104},{48,48},{56,120},{64... | collective-permute-start | bytes 1572872 | tf_op jit(solution)/shard_map/ppermute | solution.py:318
  17.8 45.5 %collective-permute-start.2 = (bf16[2,2,2,128,256]{4,3,2,1,0:T(8,128)(2,1)}, bf16[2,2,2,128,256]{4,3,2,1,0:T(8,128)(2,1)}, u32[]{:S(2)}, u32[]{:S(2)}) collective-permute-start(bf16[2,2,2,128,256]{4,3,2,1,0:T(8,128)(2,1)} %pad_maximum_fusion.2), channel_id=1, source_target_pairs={{0,16},{8,88},{16,32},{24,104},{32,48},{40,120},{48,0},{56,72},{64... | collective-permute-start | bytes 1572872 | tf_op jit(solution)/shard_map/ppermute | solution.py:318
  20.2 43.2 %collective-permute-start.3 = (bf16[2,2,2,128,256]{4,3,2,1,0:T(8,128)(2,1)}, bf16[2,2,2,128,256]{4,3,2,1,0:T(8,128)(2,1)}, u32[]{:S(2)}, u32[]{:S(2)}) collective-permute-start(bf16[2,2,2,128,256]{4,3,2,1,0:T(8,128)(2,1)} %pad_maximum_fusion.3), channel_id=1, source_target_pairs={{0,32},{8,104},{16,48},{24,120},{32,0},{40,72},{48,16},{56,88},{64... | collective-permute-start | bytes 1572872 | tf_op jit(solution)/shard_map/ppermute | solution.py:318
  21.9 41.5 %collective-permute-start.4 = (bf16[2,2,2,128,256]{4,3,2,1,0:T(8,128)(2,1)}, bf16[2,2,2,128,256]{4,3,2,1,0:T(8,128)(2,1)}, u32[]{:S(2)}, u32[]{:S(2)}) collective-permute-start(bf16[2,2,2,128,256]{4,3,2,1,0:T(8,128)(2,1)} %pad_maximum_fusion.4), channel_id=1, source_target_pairs={{0,48},{8,120},{16,0},{24,72},{32,16},{40,88},{48,32},{56,104},{64... | collective-permute-start | bytes 1572872 | tf_op jit(solution)/shard_map/ppermute | solution.py:318
  52.4 37.6 %all-to-all-start.2 = ((bf16[16,2,128,256]{3,2,1,0:T(8,128)(2,1)}), bf16[16,2,128,256]{3,2,1,0:T(8,128)(2,1)}, u32[]{:S(2)}, u32[]{:S(2)}) async-start(bf16[16,2,128,256]{3,2,1,0:T(8,128)(2,1)} %attention.2), calls=%async_computation.2 | async-start | bytes 4194304 | tf_op jit(solution)/shard_map/all_to_all | solution.py:310
  67.4 3.1 %collective-permute-start.5 = (bf16[16,128,256]{2,1,0:T(8,128)(2,1)S(1)}, bf16[16,128,256]{2,1,0:T(8,128)(2,1)}, u32[]{:S(2)}, u32[]{:S(2)}) collective-permute-start(bf16[16,128,256]{2,1,0:T(8,128)(2,1)S(1)} %bitcast.44), channel_id=1, source_target_pairs={{0,8},{8,0},{16,24},{24,16},{32,40},{40,32},{48,56},{56,48},{64,72... | collective-permute-start | bytes 3145736 | tf_op jit(solution)/shard_map/ppermute | solution.py:322
  90.0 51.3 %all-to-all-start.1 = ((bf16[16,2,128,256]{3,2,1,0:T(8,128)(2,1)}), bf16[16,2,128,256]{3,2,1,0:T(8,128)(2,1)}, u32[]{:S(2)}, u32[]{:S(2)}) async-start(bf16[16,2,128,256]{3,2,1,0:T(8,128)(2,1)} %attention.3), calls=%async_computation.1 | async-start | bytes 4194304 | tf_op jit(solution)/shard_map/all_to_all | solution.py:310
  107.8 33.5 %collective-permute-start.6 = (bf16[2,1,512,256]{3,2,1,0:T(8,128)(2,1)}, bf16[2,1,512,256]{3,2,1,0:T(8,128)(2,1)S(1)}, u32[]{:S(2)}, u32[]{:S(2)}) collective-permute-start(bf16[2,1,512,256]{3,2,1,0:T(8,128)(2,1)} %get-tuple-element.24), channel_id=1, source_target_pairs={{0,1},{1,2},{2,3},{3,4},{4,5},{5,6},{6,7},{8,9},{9,10},{10,11},{11... | collective-permute-start | bytes 1572872 | tf_op jit(solution)/shard_map/ppermute | solution.py:367
  111.6 29.7 %collective-permute-start.7 = (bf16[2,1,512,256]{3,2,1,0:T(8,128)(2,1)}, bf16[2,1,512,256]{3,2,1,0:T(8,128)(2,1)}, u32[]{:S(2)}, u32[]{:S(2)}) collective-permute-start(bf16[2,1,512,256]{3,2,1,0:T(8,128)(2,1)} %get-tuple-element.25), channel_id=1, source_target_pairs={{1,0},{2,1},{3,2},{4,3},{5,4},{6,5},{7,6},{9,8},{10,9},{11,10},{12... | collective-permute-start | bytes 1572872 | tf_op jit(solution)/shard_map/ppermute | solution.py:368
  141.4 0.8 copy-start

commit v3 on v2

--- a/solution.py
+++ b/solution.py
@@ -278,31 +278,6 @@
     )(clip.reshape(frames, rows, runs, share, C)).reshape(owners, frames, share, C)
 
 
-def late_cut_kernel(half_ref, clip_ref, out_ref):
-    for f in range(out_ref.shape[2]):
-        out_ref[:, :, f] = clip_ref[f]
-
-
-def late_cut(half, clip, owners):
-    frames, rows, width, _ = clip.shape
-    share = 4 * width // owners
-    runs = width // share
-    out = pl.pallas_call(
-        late_cut_kernel,
-        out_shape=jax.ShapeDtypeStruct((2, runs, frames, share, C), BF16),
-        grid_spec=pltpu.PrefetchScalarGridSpec(
-            num_scalar_prefetch=1,
-            grid=(1,),
-            in_specs=[pl.BlockSpec((frames, 2, runs, share, C), lambda i, s: (0, LATE[0] + s[0], 0, 0, 0))],
-            out_specs=pl.BlockSpec((2, runs, frames, share, C), lambda i, s: (0, 0, 0, 0, 0)),
-        ),
-        compiler_params=pltpu.CompilerParams(vmem_limit_bytes=VMEM),
-        cost_estimate=pl.CostEstimate(flops=1000, bytes_accessed=1000, transcendentals=0),
-        name="late_cut",
-    )(half, clip.reshape(frames, rows, runs, share, C))
-    return out.reshape(owners // 4, 2, frames, share, C)
-
-
 CHIPS = 8
 
 
@@ -340,13 +315,21 @@
     share = early.shape[2]
     early = early.reshape(FRAMES, share, chans)
 
-    theirs = to_sibling(late_cut((x + other).astype(jnp.int32).reshape(1) % 2, clip_late, 2 * CHIPS))
-    clip_late, theirs = lax.optimization_barrier((clip_late, theirs))
-    mine = late_cut((x + core).astype(jnp.int32).reshape(1) % 2, clip_late, 2 * CHIPS)
+    clip_late = clip_late.reshape(frames, rows, 4, share, chans)
+
+    def rows_for(half):
+        return lax.dynamic_slice_in_dim(clip_late, 2 * LATE[0] + 2 * half, 2, 1)
+
+    def pixels_for(source, to):
+        run = lax.dynamic_slice(source, (0, to // 2, to % 2 * 2, 0, 0), (frames, 1, 2, share, chans))
+        return run[:, 0].transpose(1, 0, 2, 3)
+
+    theirs = to_sibling(rows_for((x + other) % 2))
+    mine = rows_for((x + core) % 2)
     got = []
     for k in range(4):
         to = (y + k) % 4
-        got.append(to_chip(jnp.stack([pick(mine, to), pick(theirs, to)]), k))
+        got.append(to_chip(jnp.stack([pixels_for(mine, to), pixels_for(theirs, to)]), k))
 
     proj = attention(None, [early], weights, 64, 1000)
     proj_early = exchange(proj)

time: 154 us -> 153 us (level)
  Pallas kernels: 56.2 us -> 51.6 us
  waiting for transfers between devices: 45 us -> 49 us
    pallas_call x2 -> x0, Pallas kernels: 4.57 us -> none  [late_cut(): pl.pallas_call(late_cut_kernel, out_shape=jax.ShapeDtypeStruct((2, runs,...]
    all_to_all x3, waiting for transfers between devices: 17.7 us -> 21.9 us  [exchange(): return lax.all_to_all(a, 'frames', split_axis=0, concat_axis=0, tiled=True)]
    another operation x4 -> x2, local copies, waits for them, and re-layouts: 3.91 us -> 2.15 us  [local(): jnp.stack([pick(g, other, 1) for g in got])]
  transfers between devices with their start and end apart: 11 -> 11, of which waited for: 4 -> 4; matrix products, arithmetic and copies ran while one was open for 6% -> 5% of each run, Pallas kernels for 27% -> 25%
where the time goes in v3:
time: 153 us; the launch traced here: 152 us
  Pallas kernels  51.6 us (34%)
  waiting for transfers between devices  49 us (32%)
  starting transfers between devices  42.1 us (28%)
  local copies, waits for them, and re-layouts  6.39 us (4%)
  other arithmetic  2.78 us (2%)
    pallas_call x2, Pallas kernels, attention(): pl.pallas_call(functools.partial(attention_kernel, len(xs), not slots), o...  29.8 us
    all_to_all x3, starting transfers between devices, exchange(): return lax.all_to_all(a, 'frames', split_axis=0, concat_axis=0, tiled=True)  27.3 us
    ppermute x1, waiting for transfers between devices, local(): up = lax.ppermute(last, 'rows', [(i, i + 1) for i in range(size - 1)])  25.2 us
    all_to_all x3, waiting for transfers between devices, exchange(): return lax.all_to_all(a, 'frames', split_axis=0, concat_axis=0, tiled=True)  21.9 us
    pallas_call x1, Pallas kernels, conv_late(): pl.pallas_call(late_kernel, out_shape=out, grid=(frames,), in_specs=[row_...  10.8 us
    pallas_call x1, Pallas kernels, conv_early(): pl.pallas_call(early_kernel, out_shape=outs, grid=(frames,), in_specs=[ro...  8.38 us
    ppermute x4, starting transfers between devices, to_chip(): return lax.ppermute(a, 'frames', pairs)  6.15 us
    ppermute x1, starting transfers between devices, local(): down = lax.ppermute(lead, 'rows', [(i + 1, i) for i in range(size - 1)])  4.12 us
  transfers between devices with their start and end apart: 11, of which 4 were waited for; matrix products, arithmetic and copies ran while one was open for 5% of the time, Pallas kernels for 25%

profile of v3, /device:TPU:10, one launch (start us, length us, event | category | flops | bytes accessed | tf_op | source)
XLA Modules:
  0.0 152.1 jit_solution(17561690669940785404)
XLA Ops:
  0.0 2.6 %early_cut.1 = bf16[4,4,2,128,256]{4,3,2,1,0:T(8,128)(2,1)} custom-call(bf16[2,8,4,128,256]{4,3,2,1,0:T(8,128)(2,1)} %bitcast.84), custom_call_target="tpu_custom_call" | custom-call | flops 1000 | bytes 1000 | tf_op jit(solution)/shard_map/early_cut/pallas_call | solution.py:269
  2.6 1.3 constant_dynamic-slice_fusion.3
  3.9 0.1 copy.20
  4.0 0.1 collective-permute-start
  4.1 6.6 %all-to-all-start = ((bf16[16,2,128,256]{3,2,1,0:T(8,128)(2,1)}), bf16[16,2,128,256]{3,2,1,0:T(8,128)(2,1)}, u32[]{:S(2)}, u32[]{:S(2)}) async-start(bf16[16,2,128,256]{3,2,1,0:T(8,128)(2,1)} %bitcast.18), calls=%async_computation | async-start | bytes 4194304 | tf_op jit(solution)/shard_map/all_to_all | solution.py:285
  10.7 1.3 constant_dynamic-slice_fusion
  12.1 0.0 collective-permute-done
  12.1 0.1 dynamic-slice_bitcast_fusion.4
  12.2 0.1 pad_maximum_fusion.1
  12.3 1.4 collective-permute-start.1
  13.7 0.9 pad_maximum_fusion.2
  14.6 1.5 collective-permute-start.2
  16.1 0.9 pad_maximum_fusion.3
  16.9 1.1 collective-permute-start.3
  18.0 0.8 pad_maximum_fusion.4
  18.8 2.2 %collective-permute-start.4 = (bf16[2,2,2,128,256]{4,3,2,1,0:T(8,128)(2,1)}, bf16[2,2,2,128,256]{4,3,2,1,0:T(8,128)(2,1)}, u32[]{:S(2)}, u32[]{:S(2)}) collective-permute-start(bf16[2,2,2,128,256]{4,3,2,1,0:T(8,128)(2,1)} %pad_maximum_fusion.4), channel_id=1, source_target_pairs={{0,48},{8,120},{16,0},{24,72},{32,16},{40,88},{48,32},{56,104},{64... | collective-permute-start | bytes 1572872 | tf_op jit(solution)/shard_map/ppermute | solution.py:293
  21.0 16.0 %all-to-all-done = bf16[16,2,128,256]{3,2,1,0:T(8,128)(2,1)} async-done(((bf16[16,2,128,256]{3,2,1,0:T(8,128)(2,1)}), bf16[16,2,128,256]{3,2,1,0:T(8,128)(2,1)}, u32[]{:S(2)}, u32[]{:S(2)}) %all-to-all-start) | async-done | bytes 2097184 | tf_op jit(solution)/shard_map/all_to_all | solution.py:285
  37.1 14.5 %attention.2 = bf16[16,2,128,256]{3,2,1,0:T(8,128)(2,1)} custom-call(bf16[32,128,256]{2,1,0:T(8,128)(2,1)} %bitcast.19.refs_0_, bf16[256,256]{1,0:T(8,128)(2,1)} %refs_6_.2, bf16[256,256]{1,0:T(8,128)(2,1)} %refs_7_.2, bf16[256,256]{1,0:T(8,128)(2,1)} %refs_8_.1, bf16[256,256]{1,0:T(8,128)(2,1)} %refs_9_.1, ...), custom_call_target="tpu_custom_call" | custom-call | flops 1000 | bytes 1 | tf_op jit(solution)/shard_map/attention/pallas_call | solution.py:95
  51.5 11.0 %all-to-all-start.2 = ((bf16[16,2,128,256]{3,2,1,0:T(8,128)(2,1)}), bf16[16,2,128,256]{3,2,1,0:T(8,128)(2,1)}, u32[]{:S(2)}, u32[]{:S(2)}) async-start(bf16[16,2,128,256]{3,2,1,0:T(8,128)(2,1)} %attention.2), calls=%async_computation.2 | async-start | bytes 4194304 | tf_op jit(solution)/shard_map/all_to_all | solution.py:285
  62.5 0.0 collective-permute-done.1.refs_1_
  62.6 0.0 collective-permute-done.2.refs_2_
  62.6 0.0 collective-permute-done.3.refs_3_
  62.6 0.0 collective-permute-done.4.refs_4_
  62.6 1.1 dynamic-slice_bitcast_fusion.2
  63.7 1.1 dynamic-slice_bitcast_fusion
  64.7 0.1 pad_maximum_fusion
  64.9 0.7 collective-permute-start.5
  65.6 0.6 stack.122.refs_0_
  66.2 1.8 %collective-permute-done.5.refs_5_ = bf16[16,128,256]{2,1,0:T(8,128)(2,1)} collective-permute-done((bf16[16,128,256]{2,1,0:T(8,128)(2,1)S(1)}, bf16[16,128,256]{2,1,0:T(8,128)(2,1)}, u32[]{:S(2)}, u32[]{:S(2)}) %collective-permute-start.5) | collective-permute-done | bytes 1048608 | tf_op jit(solution)/shard_map/ppermute | solution.py:297
  68.0 15.4 %attention.3 = bf16[16,2,128,256]{3,2,1,0:T(8,128)(2,1)} custom-call(s32[17]{0:T(128)} %stack.122.refs_0_, bf16[2,2,2,128,256]{4,3,2,1,0:T(8,128)(2,1)} %collective-permute-done.1.refs_1_, bf16[2,2,2,128,256]{4,3,2,1,0:T(8,128)(2,1)} %collective-permute-done.2.refs_2_, bf16[2,2,2,128,256]{4,3,2,1,0:T(8,128)(2,1)} %collective-permute-done.3.refs_3_, ...), custom_call_target="tpu_custom_call" | custom-call | flops 5000000000 | bytes 5000000 | tf_op jit(solution)/shard_map/attention/pallas_call | solution.py:95
  83.3 5.9 %all-to-all-done.2.proj_ref = bf16[16,2,128,256]{3,2,1,0:T(8,128)(2,1)} async-done(((bf16[16,2,128,256]{3,2,1,0:T(8,128)(2,1)}), bf16[16,2,128,256]{3,2,1,0:T(8,128)(2,1)}, u32[]{:S(2)}, u32[]{:S(2)}) %all-to-all-start.2) | async-done | bytes 2097184 | tf_op jit(solution)/shard_map/all_to_all | solution.py:285
  89.2 9.7 %all-to-all-start.1 = ((bf16[16,2,128,256]{3,2,1,0:T(8,128)(2,1)}), bf16[16,2,128,256]{3,2,1,0:T(8,128)(2,1)}, u32[]{:S(2)}, u32[]{:S(2)}) async-start(bf16[16,2,128,256]{3,2,1,0:T(8,128)(2,1)} %attention.3), calls=%async_computation.1 | async-start | bytes 4194304 | tf_op jit(solution)/shard_map/all_to_all | solution.py:285
  98.9 8.4 %conv_early.1 = (f32[2,6,512,256]{3,2,1,0:T(8,128)}, bf16[2,1,512,256]{3,2,1,0:T(8,128)(2,1)}, bf16[2,1,512,256]{3,2,1,0:T(8,128)(2,1)}) custom-call(bf16[2,8,512,256]{3,2,1,0:T(8,128)(2,1)} %bottom_ref.3, bf16[2,8,512,256]{3,2,1,0:T(8,128)(2,1)} %bottom_ref.3, bf16[16,2,128,256]{3,2,1,0:T(8,128)(2,1)} %all-to-all-done.2.proj_ref, ...), custom_call_target="tpu_custom_call" | custom-call | flops 4831838208 | bytes 8388608 | tf_op jit(solution)/shard_map/conv_early/pallas_call | solution.py:221
  107.3 3.8 %collective-permute-start.6 = (bf16[2,1,512,256]{3,2,1,0:T(8,128)(2,1)}, bf16[2,1,512,256]{3,2,1,0:T(8,128)(2,1)S(1)}, u32[]{:S(2)}, u32[]{:S(2)}) collective-permute-start(bf16[2,1,512,256]{3,2,1,0:T(8,128)(2,1)} %get-tuple-element.20), channel_id=1, source_target_pairs={{0,1},{1,2},{2,3},{3,4},{4,5},{5,6},{6,7},{8,9},{9,10},{10,11},{11... | collective-permute-start | bytes 1572872 | tf_op jit(solution)/shard_map/ppermute | solution.py:350
  111.1 4.1 %collective-permute-start.7 = (bf16[2,1,512,256]{3,2,1,0:T(8,128)(2,1)}, bf16[2,1,512,256]{3,2,1,0:T(8,128)(2,1)}, u32[]{:S(2)}, u32[]{:S(2)}) collective-permute-start(bf16[2,1,512,256]{3,2,1,0:T(8,128)(2,1)} %get-tuple-element.21), channel_id=1, source_target_pairs={{1,0},{2,1},{3,2},{4,3},{5,4},{6,5},{7,6},{9,8},{10,9},{11,10},{12... | collective-permute-start | bytes 1572872 | tf_op jit(solution)/shard_map/ppermute | solution.py:351
  115.3 25.2 %collective-permute-done.6.up_ref = bf16[2,1,512,256]{3,2,1,0:T(8,128)(2,1)S(1)} collective-permute-done((bf16[2,1,512,256]{3,2,1,0:T(8,128)(2,1)}, bf16[2,1,512,256]{3,2,1,0:T(8,128)(2,1)S(1)}, u32[]{:S(2)}, u32[]{:S(2)}) %collective-permute-start.6) | collective-permute-done | bytes 524320 | tf_op jit(solution)/shard_map/ppermute | solution.py:350
  140.5 0.0 copy-start
  140.5 0.0 collective-permute-done.7.down_ref
  140.5 0.0 all-to-all-done.1.proj_ref
  140.5 0.8 copy-done
  141.3 10.8 %conv_late.1 = bf16[2,16,512,128]{3,2,1,0:T(8,128)(2,1)} custom-call(bf16[2,8,512,256]{3,2,1,0:T(8,128)(2,1)} %bottom_ref.3, bf16[2,8,512,256]{3,2,1,0:T(8,128)(2,1)} %bottom_ref.3, bf16[16,2,128,256]{3,2,1,0:T(8,128)(2,1)} %all-to-all-done.1.proj_ref, bf16[2,1,512,256]{3,2,1,0:T(8,128)(2,1)} %copy-done, ...), custom_call_target="tpu_custom_call" | custom-call | flops 4831838208 | bytes 8388608 | tf_op jit(solution)/shard_map/conv_late/pallas_call | solution.py:238
  (4 shorter events, 0.1 us)
Async XLA Ops:
  4.0 8.1 %collective-permute-start = (bf16[2,2,4,128,256]{4,3,0,2,1:T(8,128)(2,1)S(1)}, bf16[2,2,4,128,256]{4,3,0,2,1:T(8,128)(2,1)S(1)}, u32[]{:S(2)}, u32[]{:S(2)}) collective-permute-start(bf16[2,2,4,128,256]{4,3,0,2,1:T(8,128)(2,1)S(1)} %copy.20), channel_id=1, source_target_pairs={{0,8},{8,0},{16,24},{24,16},{32,40},{40,32},{48,56},{56,48},{64,72... | collective-permute-start | bytes 3145736 | tf_op jit(solution)/shard_map/ppermute | solution.py:297
  4.1 33.0 %all-to-all-start = ((bf16[16,2,128,256]{3,2,1,0:T(8,128)(2,1)}), bf16[16,2,128,256]{3,2,1,0:T(8,128)(2,1)}, u32[]{:S(2)}, u32[]{:S(2)}) async-start(bf16[16,2,128,256]{3,2,1,0:T(8,128)(2,1)} %bitcast.18), calls=%async_computation | async-start | bytes 4194304 | tf_op jit(solution)/shard_map/all_to_all | solution.py:285
  12.3 50.3 %collective-permute-start.1 = (bf16[2,2,2,128,256]{4,3,2,1,0:T(8,128)(2,1)S(1)}, bf16[2,2,2,128,256]{4,3,2,1,0:T(8,128)(2,1)}, u32[]{:S(2)}, u32[]{:S(2)}) collective-permute-start(bf16[2,2,2,128,256]{4,3,2,1,0:T(8,128)(2,1)S(1)} %pad_maximum_fusion.1), channel_id=1, source_target_pairs={{0,0},{8,72},{16,16},{24,88},{32,32},{40,104},{48,48},{56,120},{64... | collective-permute-start | bytes 1572872 | tf_op jit(solution)/shard_map/ppermute | solution.py:293
  14.6 47.9 %collective-permute-start.2 = (bf16[2,2,2,128,256]{4,3,2,1,0:T(8,128)(2,1)}, bf16[2,2,2,128,256]{4,3,2,1,0:T(8,128)(2,1)}, u32[]{:S(2)}, u32[]{:S(2)}) collective-permute-start(bf16[2,2,2,128,256]{4,3,2,1,0:T(8,128)(2,1)} %pad_maximum_fusion.2), channel_id=1, source_target_pairs={{0,16},{8,88},{16,32},{24,104},{32,48},{40,120},{48,0},{56,72},{64... | collective-permute-start | bytes 1572872 | tf_op jit(solution)/shard_map/ppermute | solution.py:293
  16.9 45.6 %collective-permute-start.3 = (bf16[2,2,2,128,256]{4,3,2,1,0:T(8,128)(2,1)}, bf16[2,2,2,128,256]{4,3,2,1,0:T(8,128)(2,1)}, u32[]{:S(2)}, u32[]{:S(2)}) collective-permute-start(bf16[2,2,2,128,256]{4,3,2,1,0:T(8,128)(2,1)} %pad_maximum_fusion.3), channel_id=1, source_target_pairs={{0,32},{8,104},{16,48},{24,120},{32,0},{40,72},{48,16},{56,88},{64... | collective-permute-start | bytes 1572872 | tf_op jit(solution)/shard_map/ppermute | solution.py:293
  18.8 43.7 %collective-permute-start.4 = (bf16[2,2,2,128,256]{4,3,2,1,0:T(8,128)(2,1)}, bf16[2,2,2,128,256]{4,3,2,1,0:T(8,128)(2,1)}, u32[]{:S(2)}, u32[]{:S(2)}) collective-permute-start(bf16[2,2,2,128,256]{4,3,2,1,0:T(8,128)(2,1)} %pad_maximum_fusion.4), channel_id=1, source_target_pairs={{0,48},{8,120},{16,0},{24,72},{32,16},{40,88},{48,32},{56,104},{64... | collective-permute-start | bytes 1572872 | tf_op jit(solution)/shard_map/ppermute | solution.py:293
  51.5 37.7 %all-to-all-start.2 = ((bf16[16,2,128,256]{3,2,1,0:T(8,128)(2,1)}), bf16[16,2,128,256]{3,2,1,0:T(8,128)(2,1)}, u32[]{:S(2)}, u32[]{:S(2)}) async-start(bf16[16,2,128,256]{3,2,1,0:T(8,128)(2,1)} %attention.2), calls=%async_computation.2 | async-start | bytes 4194304 | tf_op jit(solution)/shard_map/all_to_all | solution.py:285
  64.9 3.1 %collective-permute-start.5 = (bf16[16,128,256]{2,1,0:T(8,128)(2,1)S(1)}, bf16[16,128,256]{2,1,0:T(8,128)(2,1)}, u32[]{:S(2)}, u32[]{:S(2)}) collective-permute-start(bf16[16,128,256]{2,1,0:T(8,128)(2,1)S(1)} %bitcast.89), channel_id=1, source_target_pairs={{0,8},{8,0},{16,24},{24,16},{32,40},{40,32},{48,56},{56,48},{64,72... | collective-permute-start | bytes 3145736 | tf_op jit(solution)/shard_map/ppermute | solution.py:297
  89.2 51.3 %all-to-all-start.1 = ((bf16[16,2,128,256]{3,2,1,0:T(8,128)(2,1)}), bf16[16,2,128,256]{3,2,1,0:T(8,128)(2,1)}, u32[]{:S(2)}, u32[]{:S(2)}) async-start(bf16[16,2,128,256]{3,2,1,0:T(8,128)(2,1)} %attention.3), calls=%async_computation.1 | async-start | bytes 4194304 | tf_op jit(solution)/shard_map/all_to_all | solution.py:285
  107.3 33.2 %collective-permute-start.6 = (bf16[2,1,512,256]{3,2,1,0:T(8,128)(2,1)}, bf16[2,1,512,256]{3,2,1,0:T(8,128)(2,1)S(1)}, u32[]{:S(2)}, u32[]{:S(2)}) collective-permute-start(bf16[2,1,512,256]{3,2,1,0:T(8,128)(2,1)} %get-tuple-element.20), channel_id=1, source_target_pairs={{0,1},{1,2},{2,3},{3,4},{4,5},{5,6},{6,7},{8,9},{9,10},{10,11},{11... | collective-permute-start | bytes 1572872 | tf_op jit(solution)/shard_map/ppermute | solution.py:350
  111.1 29.4 %collective-permute-start.7 = (bf16[2,1,512,256]{3,2,1,0:T(8,128)(2,1)}, bf16[2,1,512,256]{3,2,1,0:T(8,128)(2,1)}, u32[]{:S(2)}, u32[]{:S(2)}) collective-permute-start(bf16[2,1,512,256]{3,2,1,0:T(8,128)(2,1)} %get-tuple-element.21), channel_id=1, source_target_pairs={{1,0},{2,1},{3,2},{4,3},{5,4},{6,5},{7,6},{9,8},{10,9},{11,10},{12... | collective-permute-start | bytes 1572872 | tf_op jit(solution)/shard_map/ppermute | solution.py:351
  140.5 0.8 copy-start
